TPU v7x, 512 devices: a whole 4x8x8 slice. The times are simulated.
512 devices in a mesh: ctx: 64 (over y, z), head: 8 (over x, core).
Axes of the slice: x: 4, y: 8, z: 8, core: 2. Of those that a mesh axis runs over, the one named last changes fastest.
Arguments:
- qkv_raw: bfloat16 [8192, 3, 2048], P('ctx', None, 'head'), may hold values from -6 to 6
- positions: int32 [8192], P('ctx'), may hold values from 0 to 8191, as said below
- filter_taps: float32 [3, 3, 2048], P(None, None, 'head'), may hold values from -1.2 to 1.2
- grad_out: bfloat16 [8192, 2048], P(('ctx', 'head')), may hold values from -6 to 6
Outputs:
- attn_out: bfloat16 [8192, 2048], P('ctx', 'head')
- qkv_grad: bfloat16 [8192, 3, 2048], P('ctx', None, 'head')
Inputs may be any that keep to these rules, and one draw needn't show every extreme that they name: Rows 128 d to 128 d + 127 hold, in increasing order, the positions of group c and then those of group 2 * 64 - 1 - c, each group being 64 consecutive positions, where c = (d + r) mod 64 with one r for the whole array; every position appears once.
All inputs are finite; a program needn't handle non-finite values.
Results may differ from a plain program's by a relative error of at most 0.03.
Values may be sent and summed in bfloat16 or wider, within the bound.
A program may use at most 64 MiB of HBM per device.

v0:
```python
import math

import jax
import jax.numpy as jnp
from jax import lax
from jax.sharding import PartitionSpec as P

HEAD_SIZE = 128


NEG_LARGE = -1e30


def extended_2(cells, sides, width):
    for axis, dim in sides:
        count = lax.axis_size(axis)
        head = lax.slice_in_dim(cells, 0, width, axis=dim)
        tail = lax.slice_in_dim(cells, cells.shape[dim] - width, cells.shape[dim], axis=dim)
        cells = jnp.concatenate(
            [
                lax.ppermute(tail, axis, [(i, (i + 1) % count) for i in range(count)]),
                cells,
                lax.ppermute(head, axis, [((i + 1) % count, i) for i in range(count)]),
            ],
            axis=dim,
        )
    return cells


def featurize(group_rows, prior_rows, filter_taps):
    rim_width = prior_rows.shape[0]
    row_count = group_rows.shape[0]
    extended = jnp.concatenate([prior_rows, group_rows], axis=0).astype(jnp.float32)
    result = jnp.zeros(group_rows.shape, jnp.float32)
    for tap_index in range(filter_taps.shape[1]):
        begin = rim_width - tap_index
        result = result + filter_taps[None, :, tap_index, :] * extended[begin : begin + row_count]
    return result


def unfeaturize(grad_rows, next_rows, filter_taps):
    row_count = grad_rows.shape[0]
    extended = jnp.concatenate([grad_rows, next_rows], axis=0)
    result = jnp.zeros(grad_rows.shape, jnp.float32)
    for tap_index in range(filter_taps.shape[1]):
        result = (
            result
            + filter_taps[None, :, tap_index, :] * extended[tap_index : tap_index + row_count]
        )
    return result


def locate_rows(first_row, row_count, group_len, pair_here, device_here, pair_count):
    row_ids = first_row + jnp.arange(row_count, dtype=jnp.int32)
    device_ids = row_ids // group_len
    pair_ids = (device_ids + pair_here - device_here) % pair_count
    offsets = row_ids % group_len
    early_pos = pair_ids * group_len + offsets
    late_pos = (2 * pair_count - 1 - pair_ids) * group_len + offsets
    return (early_pos, late_pos)


def split_product(left_wide, key_rows):
    high_part = left_wide.astype(jnp.bfloat16)
    rest_one = left_wide - high_part.astype(jnp.float32)
    middle_part = rest_one.astype(jnp.bfloat16)
    low_part = (rest_one - middle_part.astype(jnp.float32)).astype(jnp.bfloat16)
    total = jnp.einsum("hqk,khd->qhd", high_part, key_rows, preferred_element_type=jnp.float32)
    total = total + jnp.einsum(
        "hqk,khd->qhd", middle_part, key_rows, preferred_element_type=jnp.float32
    )
    return total + jnp.einsum(
        "hqk,khd->qhd", low_part, key_rows, preferred_element_type=jnp.float32
    )


def fresh_forward(row_count, head_count, head_size):
    return (
        jnp.full((head_count, row_count), NEG_LARGE, jnp.float32),
        jnp.zeros((head_count, row_count), jnp.float32),
        jnp.zeros((row_count, head_count, head_size), jnp.float32),
        jnp.zeros((row_count, head_count, head_size), jnp.float32),
        jnp.zeros((row_count, head_count, head_size), jnp.float32),
    )


def forward_update(
    carry_state, queries, query_pos, out_grads, key_rows, value_rows, key_pos, scaling
):
    running_max, running_sum, out_sum, weighted, plain_sum = carry_state
    scores = (
        jnp.einsum("qhd,khd->hqk", queries, key_rows, preferred_element_type=jnp.float32) * scaling
    )
    allowed = (key_pos[None, :] <= query_pos[:, None])[None]
    masked = jnp.where(allowed, scores, NEG_LARGE)
    new_max = jnp.maximum(running_max, jnp.max(masked, axis=2))
    factor = jnp.exp(running_max - new_max)
    weights = jnp.where(allowed, jnp.exp(masked - new_max[:, :, None]), 0.0)
    running_sum = running_sum * factor + jnp.sum(weights, axis=2)
    rescale = jnp.transpose(factor)[:, :, None]
    out_sum = out_sum * rescale + jnp.einsum(
        "hqk,khd->qhd", weights.astype(jnp.bfloat16), value_rows, preferred_element_type=jnp.float32
    )
    slopes = jnp.einsum("qhd,khd->hqk", out_grads, value_rows, preferred_element_type=jnp.float32)
    weighted = weighted * rescale + split_product(weights * slopes, key_rows)
    plain_sum = plain_sum * rescale + split_product(weights, key_rows)
    return (new_max, running_sum, out_sum, weighted, plain_sum)


def forward_finish(carry_state, out_grads, scaling):
    running_max, running_sum, out_sum, weighted, plain_sum = carry_state
    inverse = jnp.transpose(1.0 / running_sum)[:, :, None]
    attn = (out_sum * inverse).astype(jnp.bfloat16)
    log_total = jnp.transpose(running_max + jnp.log(running_sum))
    delta = jnp.sum(out_grads.astype(jnp.float32) * attn.astype(jnp.float32), axis=2)
    query_grad = scaling * (weighted - delta[:, :, None] * plain_sum) * inverse
    return (attn, log_total, delta, query_grad)


def forward_absorber(queries, out_grads, query_pos, locate, scaling):
    group_len = queries.shape[0] // 2
    head_count = queries.shape[1]
    head_size = queries.shape[2]

    def absorb(carried, block_in, first_row):
        key_block, value_block = block_in
        row_count = key_block.shape[1]
        step_rows = math.gcd(row_count, 256)

        def inner(step_index, state_pair):
            begin = step_index * step_rows
            key_part = lax.dynamic_slice_in_dim(key_block, begin, step_rows, 1).reshape(
                2, step_rows, head_count, head_size
            )
            value_part = lax.dynamic_slice_in_dim(value_block, begin, step_rows, 1).reshape(
                2, step_rows, head_count, head_size
            )
            early_pos, late_pos = locate(begin, step_rows)
            early_state, late_state = state_pair
            keys_both = key_part.reshape(2 * step_rows, head_count, head_size)
            values_both = value_part.reshape(2 * step_rows, head_count, head_size)
            pos_both = jnp.concatenate([early_pos, late_pos])
            late_state = forward_update(
                late_state,
                queries[group_len:],
                query_pos[group_len:],
                out_grads[group_len:],
                keys_both,
                values_both,
                pos_both,
                scaling,
            )
            early_state = forward_update(
                early_state,
                queries[:group_len],
                query_pos[:group_len],
                out_grads[:group_len],
                keys_both,
                values_both,
                pos_both,
                scaling,
            )
            return (early_state, late_state)

        return lax.fori_loop(0, row_count // step_rows, inner, carried)

    return absorb


def backward_update(
    grads_pair,
    key_rows,
    value_rows,
    key_pos,
    queries,
    out_grads,
    log_rows,
    delta_rows,
    query_pos,
    scaling,
):
    key_grad, value_grad = grads_pair
    scores = (
        jnp.einsum("qhd,khd->hqk", queries, key_rows, preferred_element_type=jnp.float32) * scaling
    )
    allowed = (key_pos[None, :] <= query_pos[:, None])[None]
    shifted = jnp.where(allowed, scores - jnp.transpose(log_rows)[:, :, None], NEG_LARGE)
    probs = jnp.where(allowed, jnp.exp(shifted), 0.0)
    value_grad = value_grad + jnp.einsum(
        "hqk,qhd->khd", probs.astype(jnp.bfloat16), out_grads, preferred_element_type=jnp.float32
    )
    slopes = jnp.einsum("qhd,khd->hqk", out_grads, value_rows, preferred_element_type=jnp.float32)
    dscores = (probs * (slopes - jnp.transpose(delta_rows)[:, :, None])).astype(jnp.bfloat16)
    key_grad = key_grad + jnp.einsum(
        "hqk,qhd->khd", dscores, queries, preferred_element_type=jnp.float32
    )
    return (key_grad, value_grad)


def backward_absorber(key_rows, value_rows, key_pos, locate, scaling):
    group_len = key_rows.shape[0] // 2
    head_count = key_rows.shape[1]
    head_size = key_rows.shape[2]

    def absorb(carried, block_in, first_row):
        query_block, grad_block, log_block, delta_block = block_in
        row_count = query_block.shape[1]
        step_rows = math.gcd(row_count, 256)

        def inner(step_index, grads_now):
            begin = step_index * step_rows
            query_part = lax.dynamic_slice_in_dim(query_block, begin, step_rows, 1).reshape(
                2, step_rows, head_count, head_size
            )
            grad_part = lax.dynamic_slice_in_dim(grad_block, begin, step_rows, 1).reshape(
                2, step_rows, head_count, head_size
            )
            log_part = lax.dynamic_slice_in_dim(log_block, begin, step_rows, 1)
            delta_part = lax.dynamic_slice_in_dim(delta_block, begin, step_rows, 1)
            early_pos, late_pos = locate(begin, step_rows)
            early_grads, late_grads = grads_now
            query_both = query_part.reshape(2 * step_rows, head_count, head_size)
            grad_both = grad_part.reshape(2 * step_rows, head_count, head_size)
            log_both = log_part.reshape(2 * step_rows, head_count)
            delta_both = delta_part.reshape(2 * step_rows, head_count)
            pos_both = jnp.concatenate([early_pos, late_pos])
            early_grads = backward_update(
                early_grads,
                key_rows[:group_len],
                value_rows[:group_len],
                key_pos[:group_len],
                query_both,
                grad_both,
                log_both,
                delta_both,
                pos_both,
                scaling,
            )
            late_grads = backward_update(
                late_grads,
                key_rows[group_len:],
                value_rows[group_len:],
                key_pos[group_len:],
                query_both,
                grad_both,
                log_both,
                delta_both,
                pos_both,
                scaling,
            )
            return (early_grads, late_grads)

        return lax.fori_loop(0, row_count // step_rows, inner, carried)

    return absorb


def local(qkv_raw, positions, filter_taps, grad_out):
    row_total = positions.shape[0]
    group_len = row_total // 2
    rim_width = filter_taps.shape[1] - 1
    channels = qkv_raw.shape[2]
    head_size = HEAD_SIZE
    head_count = channels // head_size
    scaling = 1.0 / math.sqrt(head_size)
    pair_count = lax.axis_size("ctx")
    device_here = lax.axis_index("ctx")
    pair_here = positions[0] // group_len

    def locate(first_row, row_count):
        return locate_rows(first_row, row_count, group_len, pair_here, device_here, pair_count)

    out_grads = lax.all_to_all(grad_out, "head", split_axis=1, concat_axis=0, tiled=True)
    early_rows = qkv_raw[:group_len]
    late_rows = qkv_raw[group_len:]
    early_tail = early_rows[group_len - rim_width :]
    late_tail = late_rows[group_len - rim_width :]
    tails = extended_2(jnp.concatenate([late_tail, early_tail], axis=0), (("ctx", 0),), rim_width)
    from_left = tails[:rim_width]
    from_right = tails[tails.shape[0] - rim_width :]
    early_prior = jnp.where(pair_here == 0, jnp.zeros_like(from_left), from_left)
    late_prior = jnp.where(pair_here == pair_count - 1, early_tail, from_right)
    featured = jnp.concatenate(
        [
            featurize(early_rows, early_prior, filter_taps),
            featurize(late_rows, late_prior, filter_taps),
        ],
        axis=0,
    ).astype(jnp.bfloat16)
    query_rows = featured[:, 0]
    key_rows = featured[:, 1]
    value_rows = featured[:, 2]
    col_first = 0 * head_size
    col_last = col_first + head_count * head_size
    width_now = col_last - col_first
    query_heads = query_rows.reshape(row_total, head_count, head_size)
    grad_heads = out_grads.reshape(row_total, head_count, head_size)
    initial = (
        fresh_forward(group_len, head_count, head_size),
        fresh_forward(group_len, head_count, head_size),
    )
    absorb = forward_absorber(query_heads, grad_heads, positions, locate, scaling)
    early_state, late_state = absorb(
        initial,
        (
            lax.all_gather(key_rows.reshape(2, group_len, width_now), "ctx", axis=1, tiled=True),
            lax.all_gather(value_rows.reshape(2, group_len, width_now), "ctx", axis=1, tiled=True),
        ),
        jnp.int32(0),
    )
    early_out = forward_finish(early_state, grad_heads[:group_len], scaling)
    late_out = forward_finish(late_state, grad_heads[group_len:], scaling)
    attn = jnp.concatenate([early_out[0], late_out[0]], axis=0)
    log_total = jnp.concatenate([early_out[1], late_out[1]], axis=0)
    delta = jnp.concatenate([early_out[2], late_out[2]], axis=0)
    query_grad = jnp.concatenate([early_out[3], late_out[3]], axis=0)
    absorb_back = backward_absorber(
        key_rows.reshape(row_total, head_count, head_size),
        value_rows.reshape(row_total, head_count, head_size),
        positions,
        locate,
        scaling,
    )
    zero_grads = (
        jnp.zeros((group_len, head_count, head_size), jnp.float32),
        jnp.zeros((group_len, head_count, head_size), jnp.float32),
    )
    early_grads, late_grads = absorb_back(
        (zero_grads, zero_grads),
        (
            lax.all_gather(
                query_rows.reshape(2, group_len, width_now).astype(jnp.float32),
                "ctx",
                axis=1,
                tiled=True,
            ).astype(jnp.bfloat16),
            lax.all_gather(
                out_grads.reshape(2, group_len, width_now).astype(jnp.float32),
                "ctx",
                axis=1,
                tiled=True,
            ).astype(jnp.bfloat16),
            lax.all_gather(log_total.reshape(2, group_len, head_count), "ctx", axis=1, tiled=True),
            lax.all_gather(delta.reshape(2, group_len, head_count), "ctx", axis=1, tiled=True),
        ),
        jnp.int32(0),
    )
    key_grad = scaling * jnp.concatenate([early_grads[0], late_grads[0]], axis=0)
    value_grad = jnp.concatenate([early_grads[1], late_grads[1]], axis=0)
    results = [(attn, query_grad, key_grad, value_grad)]
    attn_all = jnp.concatenate([entry[0] for entry in results], axis=1).reshape(row_total, channels)
    query_grad_all = jnp.concatenate([entry[1] for entry in results], axis=1).reshape(
        row_total, channels
    )
    key_grad_all = jnp.concatenate([entry[2] for entry in results], axis=1).reshape(
        row_total, channels
    )
    value_grad_all = jnp.concatenate([entry[3] for entry in results], axis=1).reshape(
        row_total, channels
    )
    post_grads = jnp.stack([query_grad_all, key_grad_all, value_grad_all], axis=1)
    early_head = post_grads[:rim_width]
    late_head = post_grads[group_len : group_len + rim_width]
    heads_rim = extended_2(
        jnp.concatenate([early_head, late_head], axis=0), (("ctx", 0),), rim_width
    )
    grad_left = heads_rim[:rim_width]
    grad_right = heads_rim[heads_rim.shape[0] - rim_width :]
    early_next = jnp.where(pair_here == pair_count - 1, late_head, grad_right)
    late_next = jnp.where(pair_here == 0, jnp.zeros_like(grad_left), grad_left)
    raw_grads = jnp.concatenate(
        [
            unfeaturize(post_grads[:group_len], early_next, filter_taps),
            unfeaturize(post_grads[group_len:], late_next, filter_taps),
        ],
        axis=0,
    )
    return (attn_all, raw_grads.astype(jnp.bfloat16))


def solution(mesh):
    in_specs = (P("ctx", None, "head"), P("ctx"), P(None, None, "head"), P(("ctx", "head"), None))
    out_specs = (P("ctx", "head"), P("ctx", None, "head"))
    return jax.shard_map(local, mesh=mesh, in_specs=in_specs, out_specs=out_specs, check_vma=False)
```

profile of v0, /device:TPU:6, one launch (start us, length us, event | category | flops | bytes accessed | tf_op | source)
XLA Modules:
  0.0 526.3 jit_solution(4368539386016358668)
XLA Ops:
  7.9 13.8 %collective-permute-start.1 = (bf16[2,3,256]{2,0,1:T(2,128)(2,1)S(1)}, bf16[2,3,256]{2,0,1:T(2,128)(2,1)S(1)}, u32[]{:S(2)}, u32[]{:S(2)}) collective-permute-start(bf16[2,3,256]{2,0,1:T(2,128)(2,1)S(1)} %slice.223), channel_id=1, source_target_pairs={{8,0},{16,8},{24,16},{32,24},{40,32},{48,40},{56,48},{64,56},{72,6... | collective-permute-start | bytes 9224 | tf_op jit(solution)/shard_map/ppermute | solution.py:23
  26.9 1.9 collective-permute-start
  28.9 6.8 %collective-permute-done = bf16[2,3,256]{2,0,1:T(2,128)(2,1)S(1)} collective-permute-done((bf16[2,3,256]{2,0,1:T(2,128)(2,1)S(1)}, bf16[2,3,256]{2,0,1:T(2,128)(2,1)S(1)}, u32[]{:S(2)}, u32[]{:S(2)}) %collective-permute-start) | collective-permute-done | bytes 3104 | tf_op jit(solution)/shard_map/ppermute | solution.py:21
  38.1 1.5 copy.311
  39.6 4.8 all-to-all-start
  48.6 68.4 %all-gather.5.cloned.1.call-done = bf16[2,4096,256]{2,1,0:T(8,128)(2,1)} async-done(((bf16[2,64,256]{2,1,0:T(8,128)(2,1)}), bf16[2,4096,256]{2,1,0:T(8,128)(2,1)}) %all-gather.5.cloned.1.call-update) | async-done | bytes 4194320 | tf_op jit(solution)/shard_map/all_gather | solution.py:306
  117.0 87.5 %all-gather.7.cloned.1.call-done = bf16[2,4096,256]{2,1,0:T(8,128)(2,1)} async-done(((bf16[2,64,256]{2,1,0:T(8,128)(2,1)}), bf16[2,4096,256]{2,1,0:T(8,128)(2,1)}) %all-gather.7.cloned.1.call-update) | async-done | bytes 4194320 | tf_op jit(solution)/shard_map/all_gather | solution.py:307
  204.5 114.2 %while.56 = (s32[]{:T(128)}, f32[2,64]{1,0:T(2,128)S(1)}, f32[2,64]{1,0:T(2,128)S(1)}, f32[64,2,128]{2,0,1:T(8,128)S(1)}, f32[64,2,128]{2,0,1:T(8,128)S(1)}, /*i...) while((s32[]{:T(128)}, f32[2,64]{1,0:T(2,128)S(1)}, ...), condition=%wide.region_5.6_spmd.clone, body=%wide.region_0.5_spmd.clone.sunk | while | flops 308006656 | bytes 15106853 | solution.py:165
  320.3 66.4 %all_gather.23 = f32[2,4096,2]{2,0,1:T(2,128)} all-gather(f32[2,64,2]{2,0,1:T(2,128)S(1)} %copy.224), channel_id=1, replica_groups=mesh['ctx'=64,'head'=8] {'ctx'}, dimensions={1}, use_global_device_ids=true | all-gather | bytes 66560 | tf_op jit(solution)/shard_map/all_gather | solution.py:344
  386.7 5.2 copy.228
  392.2 56.0 %all_gather.21 = f32[2,4096,2]{2,0,1:T(2,128)} all-gather(f32[2,64,2]{2,0,1:T(2,128)S(1)} %copy.221), channel_id=1, replica_groups=mesh['ctx'=64,'head'=8] {'ctx'}, dimensions={1}, use_global_device_ids=true | all-gather | bytes 66560 | tf_op jit(solution)/shard_map/all_gather | solution.py:343
  448.2 5.2 copy.226
  454.1 49.3 %while.57 = (s32[]{:T(128)}, f32[64,2,128]{2,0,1:T(8,128)S(1)}, f32[64,2,128]{2,0,1:T(8,128)S(1)}, f32[64,2,128]{2,0,1:T(8,128)S(1)}, f32[64,2,128]{2,0,1:T(8,12...) while((s32[]{:T(128)}, f32[64,2,128]{2,0,1:T(8,128)S(1)}, ...), condition=%wide.region_9.10_spmd.clone, body=%wide.region_8.9_spmd.clone.sunk | while | flops 135473152 | bytes 6612724 | solution.py:253
  457.1 1.1 constant_dynamic-slice_fusion.9
  460.2 1.1 constant_dynamic-slice_fusion.9
  463.3 1.1 constant_dynamic-slice_fusion.9
  466.4 1.1 constant_dynamic-slice_fusion.9
  469.5 1.1 constant_dynamic-slice_fusion.9
  472.6 1.1 constant_dynamic-slice_fusion.9
  475.6 1.1 constant_dynamic-slice_fusion.9
  478.7 1.1 constant_dynamic-slice_fusion.9
  481.8 1.1 constant_dynamic-slice_fusion.9
  484.9 1.1 constant_dynamic-slice_fusion.9
  488.0 1.1 constant_dynamic-slice_fusion.9
  491.1 1.1 constant_dynamic-slice_fusion.9
  494.2 1.1 constant_dynamic-slice_fusion.9
  497.2 1.1 constant_dynamic-slice_fusion.9
  500.3 1.1 constant_dynamic-slice_fusion.9
  503.9 4.6 collective-permute-start.2
  508.5 1.3 collective-permute-done.2
  509.8 2.3 collective-permute-start.3
  512.2 6.8 %collective-permute-done.3 = f32[2,3,256]{2,0,1:T(2,128)S(1)} collective-permute-done((f32[2,3,256]{2,0,1:T(2,128)S(1)}, f32[2,3,256]{2,0,1:T(2,128)S(1)}, u32[]{:S(2)}, u32[]{:S(2)}) %collective-permute-start.3) | collective-permute-done | bytes 6176 | tf_op jit(solution)/shard_map/ppermute | solution.py:21
  (875 shorter events, 156.1 us)
Async XLA Ops:
  7.2 197.3 %copy-start.1 = (s32[128]{0:T(128)S(1)}, s32[128]{0:T(128)}, u32[]{:S(2)}) copy-start(s32[128]{0:T(128)} %param.9) | copy-start | bytes 1540
  7.2 109.8 %all-gather.5.cloned.1.call-start = ((), (), s32[]{:S(2)}) async-start(), calls=%async_computation.1 | async-start | bytes 4259840 | tf_op jit(solution)/shard_map/all_gather | solution.py:306
  7.9 18.3 %collective-permute-start.1 = (bf16[2,3,256]{2,0,1:T(2,128)(2,1)S(1)}, bf16[2,3,256]{2,0,1:T(2,128)(2,1)S(1)}, u32[]{:S(2)}, u32[]{:S(2)}) collective-permute-start(bf16[2,3,256]{2,0,1:T(2,128)(2,1)S(1)} %slice.223), channel_id=1, source_target_pairs={{8,0},{16,8},{24,16},{32,24},{40,32},{48,40},{56,48},{64,56},{72,6... | collective-permute-start | bytes 9224 | tf_op jit(solution)/shard_map/ppermute | solution.py:23
  26.9 8.8 %collective-permute-start = (bf16[2,3,256]{2,0,1:T(2,128)(2,1)S(1)}, bf16[2,3,256]{2,0,1:T(2,128)(2,1)S(1)}, u32[]{:S(2)}, u32[]{:S(2)}) collective-permute-start(bf16[2,3,256]{2,0,1:T(2,128)(2,1)S(1)} %get-tuple-element.1180), channel_id=1, source_target_pairs={{0,8},{8,16},{16,24},{24,32},{32,40},{40,48},{48,56},{56,64},{64,7... | collective-permute-start | bytes 9224 | tf_op jit(solution)/shard_map/ppermute | solution.py:21
  36.6 167.9 %all-gather.7.cloned.1.call-start = ((), (), s32[]{:S(2)}) async-start(), calls=%async_computation.2 | async-start | bytes 4259840 | tf_op jit(solution)/shard_map/all_gather | solution.py:307
  37.4 416.7 %all-gather.9.cloned.1.call-start = ((), (), s32[]{:S(2)}) async-start(), calls=%async_computation.3 | async-start | bytes 4259840 | tf_op jit(solution)/shard_map/all_gather | solution.py:331
  39.6 8.3 %all-to-all-start = ((bf16[16,8,256]{2,0,1:T(8,128)(2,1)}), bf16[16,8,256]{2,0,1:T(8,128)(2,1)S(1)}, u32[]{:S(2)}, u32[]{:S(2)}) async-start(bf16[16,8,256]{2,0,1:T(8,128)(2,1)} %bitcast.116), calls=%async_computation | async-start | bytes 131072 | tf_op jit(solution)/shard_map/all_to_all | solution.py:273
  44.4 409.7 %all-gather.11.cloned.1.call-start = ((), (), s32[]{:S(2)}) async-start(), calls=%async_computation.4 | async-start | bytes 4259840 | tf_op jit(solution)/shard_map/all_gather | solution.py:337
  47.9 0.6 copy-start
  503.9 5.9 %collective-permute-start.2 = (f32[2,3,256]{2,0,1:T(2,128)S(1)}, f32[2,3,256]{2,0,1:T(2,128)S(1)}, u32[]{:S(2)}, u32[]{:S(2)}) collective-permute-start(f32[2,3,256]{2,0,1:T(2,128)S(1)} %pad_maximum_fusion.8), channel_id=1, source_target_pairs={{8,0},{16,8},{24,16},{32,24},{40,32},{48,40},{56,48},{64,56},{72,6... | collective-permute-start | bytes 18440 | tf_op jit(solution)/shard_map/ppermute | solution.py:23
  509.8 9.1 %collective-permute-start.3 = (f32[2,3,256]{2,0,1:T(2,128)S(1)}, f32[2,3,256]{2,0,1:T(2,128)S(1)}, u32[]{:S(2)}, u32[]{:S(2)}) collective-permute-start(f32[2,3,256]{2,0,1:T(2,128)S(1)} %get-tuple-element.1145), channel_id=1, source_target_pairs={{0,8},{8,16},{16,24},{24,32},{32,40},{40,48},{48,56},{56,64},{64,7... | collective-permute-start | bytes 18440 | tf_op jit(solution)/shard_map/ppermute | solution.py:21
Sparse Core Ops, SparseCore 0:
  36.8 80.1 all-gather.4
  120.6 83.8 all-gather.6
  207.6 84.2 all-gather.8
  294.8 92.3 all-gather.10
where the time goes:
time: 529 us; the launch traced here: 526 us
  waiting for transfers between devices  173 us (33%)
  blocking collectives  122 us (23%)
  matrix products  91.4 us (17%)
  local copies, waits for them, and re-layouts  75.1 us (14%)
  starting transfers between devices  27.5 us (5%)
  between operations  16.8 us (3%)
  other arithmetic  15.2 us (3%)
    all_gather x1, waiting for transfers between devices, local(): lax.all_gather(value_rows.reshape(2, group_len, width_now), 'ctx', axis=1...  87.5 us
    all_gather x1, waiting for transfers between devices, local(): lax.all_gather(key_rows.reshape(2, group_len, width_now), 'ctx', axis=1,...  68.4 us
    all_gather x1, blocking collectives, local(): lax.all_gather(delta.reshape(2, group_len, head_count), 'ctx', axis=1, ti...  66.4 us
    all_gather x1, blocking collectives, local(): lax.all_gather(log_total.reshape(2, group_len, head_count), 'ctx', axis=1...  56 us
    ppermute x2, starting transfers between devices, extended_2(): lax.ppermute(head, axis, [((i + 1) % count, i) for i in range(count)])  18.4 us
    dynamic_slice x16, local copies, waits for them, and re-layouts, inner(): lax.dynamic_slice_in_dim(grad_block, begin, step_rows, 1)  17.2 us
    dynamic_slice x16, local copies, waits for them, and re-layouts, inner(): lax.dynamic_slice_in_dim(value_block, begin, step_rows, 1)  15.7 us
    dynamic_slice x16, local copies, waits for them, and re-layouts, inner(): lax.dynamic_slice_in_dim(key_block, begin, step_rows, 1)  15.6 us
  transfers between devices with their start and end apart: 9, of which 6 were waited for; matrix products, arithmetic and copies ran while one was open for 25% of the time, Pallas kernels for 0%

commit v1 on v0

v1 whole, which is shorter than its diff:
```python
import functools
import math

import jax
import jax.numpy as jnp
from jax import lax
from jax.experimental import pallas as pl
from jax.experimental.pallas import tpu as pltpu
from jax.sharding import PartitionSpec as P

HD = 128
MESH = pl.DeviceIdType.MESH
NEG = -1e30
F32 = jnp.float32
BF16 = jnp.bfloat16


def kernel(
    dims,
    raw_ref,
    pos_ref,
    taps_ref,
    gout_ref,
    attn_ref,
    grad_ref,
    land,
    halo_raw,
    q_all,
    d_all,
    k_all,
    v_all,
    k_code,
    w_all,
    s_all,
    p_low,
    x_low,
    stats,
    row_fac,
    row_del,
    part_o,
    part_q,
    part_k,
    part_v,
    rs_out,
    rs_in,
    fin,
    halo_out,
    halo_in,
    own_sem,
    a2a_send,
    a2a_recv,
    hr_send,
    hr_recv,
    ag_send,
    ag_recv,
    st_send,
    st_recv,
    rs_send,
    rs_recv,
    hg_send,
    hg_recv,
):
    Y, Z, H, G, NH, T = dims
    N = Y * Z
    d = lax.axis_index("ctx")
    hd = lax.axis_index("head")
    y = d // Z
    z = d % Z
    scaling = 1.0 / math.sqrt(HD)
    cexp = scaling * math.log2(math.e)

    d_next = (d + 1) % N
    d_prev = (d + N - 1) % N
    z_dev = lambda i: y * Z + i
    y_dev = lambda i: i * Z + z

    barrier = pltpu.get_barrier_semaphore()
    greet = [(z_dev((z + j) % Z), hd) for j in range(1, Z)]
    greet += [(y_dev((y + 1) % Y), hd), (y_dev((y + Y - 1) % Y), hd)]
    greet += [(d_next, hd), (d_prev, hd)]
    greet += [(d, (hd + j) % H) for j in range(1, H)]
    for dev in greet:
        pl.semaphore_signal(barrier, inc=1, device_id=dev, device_id_type=MESH)
    pl.semaphore_wait(barrier, len(greet))

    def remote(src, dst, s_sem, r_sem, dev):
        return pltpu.make_async_remote_copy(
            src_ref=src, dst_ref=dst, send_sem=s_sem, recv_sem=r_sem, device_id=dev, device_id_type=MESH
        )

    tail_e = remote(
        raw_ref.at[:, pl.ds(G - 16, 16)], halo_raw.at[0], hr_send.at[0], hr_recv.at[0], (d_next, hd)
    )
    tail_l = remote(
        raw_ref.at[:, pl.ds(2 * G - 16, 16)], halo_raw.at[1], hr_send.at[1], hr_recv.at[1], (d_prev, hd)
    )
    tail_e.start()
    tail_l.start()
    RB = 2 * G // H
    CW = NH * HD

    def a2a(j):
        to = (hd + j) % H
        return remote(
            gout_ref.at[:, pl.ds(pl.multiple_of(to * CW, CW), CW)],
            land.at[pl.ds(pl.multiple_of(hd * RB, RB), RB)],
            a2a_send.at[j - 1],
            a2a_recv.at[j - 1],
            (d, to),
        )

    def a2a_in(j):
        frm = (hd + H - j) % H
        return remote(
            gout_ref.at[:, pl.ds(pl.multiple_of(hd * CW, CW), CW)],
            land.at[pl.ds(pl.multiple_of(frm * RB, RB), RB)],
            a2a_send.at[j - 1],
            a2a_recv.at[j - 1],
            (d, frm),
        )

    for j in range(1, H):
        a2a(j).start()
    own = pltpu.make_async_copy(
        gout_ref.at[:, pl.ds(pl.multiple_of(hd * CW, CW), CW)],
        land.at[pl.ds(pl.multiple_of(hd * RB, RB), RB)],
        own_sem,
    )
    own.start()

    pair = pos_ref[0] // G
    rot = (pair - d + N) % N
    nk = Y * G
    nq = Z * G
    C = min(256, nq)
    ik = lax.broadcasted_iota(jnp.int32, (nk, C), 0)
    pk = ((ik // G) * Z + (z + rot)) % N
    k_code[0] = pk * G + ik % G
    k_code[1] = ik % G - pk * G

    def q_code(half, c):
        iq = lax.broadcasted_iota(jnp.int32, (1, C), 1) + c * C
        pq = (iq // G + (y * Z + rot)) % N
        return pq * G + iq % G if half == 0 else iq % G - pq * G

    rings = [
        (q_all, Z, z, z_dev, 0),
        (d_all, Z, z, z_dev, 1),
        (k_all, Y, y, y_dev, 0),
        (v_all, Y, y, y_dev, 1),
    ]

    def steps_of(n, flip):
        a, b = n // 2, n - 1 - n // 2
        return (b, a) if flip else (a, b)

    MR = max(Y, Z) // 2

    def ag_copy(h, item, way, s):
        buf, n, me, dev_of, flip = rings[item]
        sign = 1 if way == 0 else n - 1
        slot = (me + (n - sign) * s) % n
        dev = (dev_of((me + sign) % n), hd)
        return remote(
            buf.at[h, :, slot], buf.at[h, :, slot], ag_send.at[h, item, way, s], ag_recv.at[h, item, way, s], dev
        )

    def ag_wait(h, item, way, s):
        buf, n, me, dev_of, flip = rings[item]
        sign = 1 if way == 0 else n - 1
        slot = (me + (n - sign) * (s + 1)) % n
        dev = (dev_of((me + sign) % n), hd)
        remote(
            buf.at[h, :, slot], buf.at[h, :, slot], ag_send.at[h, item, way, s], ag_recv.at[h, item, way, s], dev
        ).wait_recv()

    def ag_round(h, s, items=(2, 0, 3, 1)):
        for item in items:
            n, flip = rings[item][1], rings[item][4]
            steps = steps_of(n, flip)
            for way in range(2):
                if 0 < s <= steps[way]:
                    ag_wait(h, item, way, s - 1)
                if s < steps[way]:
                    ag_copy(h, item, way, s).start()

    tail_e.wait_recv()
    tail_l.wait_recv()
    row = lax.broadcasted_iota(jnp.int32, (G, CW), 0)
    zero_rows = jnp.zeros((16, CW), F32)

    def featurize(kind, half):
        x = raw_ref[kind, pl.ds(half * G, G)].astype(F32)
        if half == 0:
            prior = jnp.where(pair == 0, zero_rows, halo_raw[0, kind].astype(F32))
        else:
            prior = jnp.where(
                pair == N - 1, raw_ref[kind, pl.ds(G - 16, 16)].astype(F32), halo_raw[1, kind].astype(F32)
            )
        tap = taps_ref[kind]
        out = tap[0:1] * x
        for t in range(1, T):
            moved = pltpu.roll(x, t, 0)
            for i in range(t):
                moved = jnp.where(row == i, prior[16 - t + i : 17 - t + i], moved)
            out = out + tap[t : t + 1] * moved
        return out.astype(BF16)

    for kind, buf, slot in ((1, k_all, y), (0, q_all, z), (2, v_all, y)):
        for half in range(2):
            out = featurize(kind, half)
            for h in range(NH):
                buf[h, half, slot] = out[:, h * HD : (h + 1) * HD]
        ag_round(0, 0, ((1, 2), (0, 0), (2, 3))[(1, 0, 2).index(kind)][1:])
    own.wait()
    for j in range(1, H):
        a2a_in(j).wait_recv()
    for half in range(2):
        for h in range(NH):
            d_all[h, half, z] = land[pl.ds(half * G, G), h * HD : (h + 1) * HD]
    ag_round(0, 0, (1,))

    NT = (((1,), (1,)), ((), ()))
    TN = (((0,), (0,)), ((), ()))
    NN = (((1,), (0,)), ((), ()))

    def mm(a, b, how):
        return lax.dot_general(a, b, how, preferred_element_type=F32)

    zc = C // G
    lanes = C // 128

    def pass1(h, half, c):
        q = q_all[h, half, pl.ds(c * zc, zc)].reshape(C, HD)
        g = d_all[h, half, pl.ds(c * zc, zc)].reshape(C, HD)
        cols = pl.ds(half * nq + c * C, C)
        tops = []
        score = []
        for kh in range(half + 1):
            keys = k_all[h, kh].reshape(nk, HD)
            sc = mm(keys, q, NT)
            if kh == half:
                sc = jnp.where(k_code[half] <= q_code(half, c), sc, NEG)
            score.append(sc)
            tops.append(jnp.max(sc, axis=0, keepdims=True))
        top = tops[0] if half == 0 else jnp.maximum(tops[0], tops[1])
        total = jnp.zeros((1, C), F32)
        tilt = jnp.zeros((1, C), F32)
        for kh in range(half + 1):
            w = jnp.exp2((score[kh] - top) * cexp)
            w_all[h, pl.ds(kh * nk, nk), cols] = w
            slope = mm(v_all[h, kh].reshape(nk, HD), g, NT)
            s_all[h, pl.ds(kh * nk, nk), cols] = slope
            total = total + jnp.sum(w, axis=0, keepdims=True)
            tilt = tilt + jnp.sum(w * slope, axis=0, keepdims=True)
        for i in range(lanes):
            r = (half * nq + c * C) // 128 + i
            for what, val in enumerate((top, total, tilt)):
                stats[h, z, what, pl.ds(r, 1)] = val[:, i * 128 : (i + 1) * 128]

    def st_copy(h, j, incoming=False):
        slot = (z + Z - j) % Z if incoming else z
        dev = z_dev((z + Z - j) % Z if incoming else (z + j) % Z)
        return remote(stats.at[h, slot], stats.at[h, slot], st_send.at[h, j - 1], st_recv.at[h, j - 1], (dev, hd))

    def st_start(h):
        for j in range(1, Z):
            st_copy(h, j).start()

    def st_finish(h):
        for j in range(1, Z):
            st_copy(h, j, True).wait_recv()
        top = stats[h, 0, 0]
        for i in range(1, Z):
            top = jnp.maximum(top, stats[h, i, 0])
        total = jnp.zeros_like(top)
        tilt = jnp.zeros_like(top)
        for i in range(Z):
            e = jnp.exp2((stats[h, i, 0] - top) * cexp)
            total = total + stats[h, i, 1] * e
            tilt = tilt + stats[h, i, 2] * e
        inv = 1.0 / total
        row_fac[h] = jnp.exp2((stats[h, z, 0] - top) * cexp) * inv
        row_del[h] = tilt * inv

    nr = 2 * nq // 128

    def row_of(ref, h, a, b):
        return jnp.concatenate([ref[h, pl.ds(i, 1)] for i in range(a // 128, b // 128)], axis=1)

    KC = min(256, nk)
    kz = KC // G

    def pass2_keys(h, kh, c):
        rows = pl.ds(kh * nk + c * KC, KC)
        lo = 0 if kh == 0 else nq
        cols = pl.ds(lo, 2 * nq - lo)
        fac = row_of(row_fac, h, lo, 2 * nq)
        dl = row_of(row_del, h, lo, 2 * nq)
        p = w_all[h, rows, cols] * fac
        pb = p.astype(BF16)
        p_low[rows, cols] = pb
        xb = (p * (s_all[h, rows, cols] - dl)).astype(BF16)
        x_low[rows, cols] = xb
        if kh == 0:
            g = d_all[h].reshape(2 * nq, HD)
            q = q_all[h].reshape(2 * nq, HD)
        else:
            g = d_all[h, 1].reshape(nq, HD)
            q = q_all[h, 1].reshape(nq, HD)
        part_v[h, kh, pl.ds(c * kz, kz)] = mm(pb, g, NN).reshape(kz, G, HD)
        part_k[h, kh, pl.ds(c * kz, kz)] = (mm(xb, q, NN) * scaling).reshape(kz, G, HD)

    def pass2_queries(h, half):
        ks = pl.ds(0, nk * (half + 1))
        cols = pl.ds(half * nq, nq)
        if half == 0:
            k = k_all[h, 0].reshape(nk, HD)
            v = v_all[h, 0].reshape(nk, HD)
        else:
            k = k_all[h].reshape(2 * nk, HD)
            v = v_all[h].reshape(2 * nk, HD)
        part_o[h, half] = mm(p_low[ks, cols], v, TN).reshape(Z, G, HD)
        part_q[h, half] = (mm(x_low[ks, cols], k, TN) * scaling).reshape(Z, G, HD)

    rs_rings = [
        (part_o, Z, z, z_dev, 0),
        (part_q, Z, z, z_dev, 1),
        (part_k, Y, y, y_dev, 0),
        (part_v, Y, y, y_dev, 1),
    ]

    def rs_copy(h, item, way, s):
        part, n, me, dev_of, flip = rs_rings[item]
        sign = 1 if way == 0 else n - 1
        return remote(
            rs_out.at[h, item, way, s],
            rs_in.at[h, item, way, s],
            rs_send.at[h, item, way, s],
            rs_recv.at[h, item, way, s],
            (dev_of((me + sign) % n), hd),
        )

    def rs_round(h, s, items=(2, 0, 3, 1)):
        for item in items:
            part, n, me, dev_of, flip = rs_rings[item]
            steps = steps_of(n, flip)
            for way in range(2):
                count = steps[way]
                if s < count:
                    sign = 1 if way == 0 else n - 1
                    dest = (me + sign * (count - s)) % n
                    val = part[h, :, pl.ds(dest, 1)].reshape(2, G, HD)
                    if s > 0:
                        rs_copy(h, item, way, s - 1).wait_recv()
                        val = val + rs_in[h, item, way, s - 1].astype(F32)
                    rs_out[h, item, way, s] = val.astype(BF16)
                    rs_copy(h, item, way, s).start()

    def rs_final(h, item):
        part, n, me, dev_of, flip = rs_rings[item]
        steps = steps_of(n, flip)
        val = part[h, :, pl.ds(me, 1)].reshape(2, G, HD)
        for way in range(2):
            if steps[way] > 0:
                rs_copy(h, item, way, steps[way] - 1).wait_recv()
                val = val + rs_in[h, item, way, steps[way] - 1].astype(F32)
        return val

    def hg_copy(h, half):
        return remote(
            halo_out.at[h, half],
            halo_in.at[h, half],
            hg_send.at[h, half],
            hg_recv.at[h, half],
            (d_prev if half == 0 else d_next, hd),
        )

    def finish_sums(h):
        for kind, item in ((0, 1), (1, 2), (2, 3)):
            val = rs_final(h, item)
            fin[h, kind] = val
            for half in range(2):
                halo_out[h, half, kind] = val[half, 0:8]
        for half in range(2):
            hg_copy(h, half).start()
        o = rs_final(h, 0).astype(BF16)
        for half in range(2):
            attn_ref[pl.ds(half * G, G), h * HD : (h + 1) * HD] = o[half]

    row1 = lax.broadcasted_iota(jnp.int32, (G, HD), 0)

    def finish_grads(h):
        for half in range(2):
            hg_copy(h, half).wait_recv()
        for kind in range(3):
            tap = taps_ref[kind][:, h * HD : (h + 1) * HD]
            for half in range(2):
                x = fin[h, kind, half]
                if half == 0:
                    nxt = jnp.where(pair == N - 1, fin[h, kind, 1, 0:8], halo_in[h, 0, kind])
                else:
                    nxt = jnp.where(pair == 0, jnp.zeros((8, HD), F32), halo_in[h, 1, kind])
                out = tap[0:1] * x
                for t in range(1, T):
                    moved = pltpu.roll(x, G - t, 0)
                    for i in range(t):
                        moved = jnp.where(row1 == G - t + i, nxt[i : i + 1], moved)
                    out = out + tap[t : t + 1] * moved
                grad_ref[kind, pl.ds(half * G, G), h * HD : (h + 1) * HD] = out.astype(BF16)

    nc = nq // C
    kc = nk // KC
    chunks = [(1, c) for c in range(nc)] + [(0, c) for c in range(nc)]
    for s in range(1, MR + 1):
        if s == min(3, MR):
            ag_round(1, 0)
        ag_round(0, s)
    done = 1
    for half, c in chunks:
        if done < MR:
            ag_round(1, done)
            done += 1
        pass1(0, half, c)
    while done <= MR:
        ag_round(1, done)
        done += 1
    st_start(0)
    for half, c in chunks:
        pass1(1, half, c)
    st_start(1)
    st_finish(0)
    for kh in range(2):
        for c in range(kc):
            pass2_keys(0, kh, c)
    rs_round(0, 0, (2, 3))
    for half in range(2):
        pass2_queries(0, half)
    rs_round(0, 0, (0, 1))
    st_finish(1)
    done = 1
    for kh in range(2):
        for c in range(kc):
            pass2_keys(1, kh, c)
            if done < MR:
                rs_round(0, done)
                done += 1
    rs_round(1, 0, (2, 3))
    for half in range(2):
        pass2_queries(1, half)
    rs_round(1, 0, (0, 1))
    while done < MR:
        rs_round(0, done)
        done += 1
    finish_sums(0)
    for s in range(1, MR):
        rs_round(1, s)
    finish_sums(1)
    finish_grads(0)
    finish_grads(1)

    tail_e.wait_send()
    tail_l.wait_send()
    for j in range(1, H):
        a2a(j).wait_send()
    for h in range(NH):
        for item in range(4):
            n, flip = rings[item][1], rings[item][4]
            steps = steps_of(n, flip)
            for way in range(2):
                for s in range(steps[way]):
                    ag_copy(h, item, way, s).wait_send()
                    rs_copy(h, item, way, s).wait_send()
        for j in range(1, Z):
            st_copy(h, j).wait_send()
        for half in range(2):
            hg_copy(h, half).wait_send()


def local(Y, Z, H, qkv_raw, positions, filter_taps, grad_out):
    rows = positions.shape[0]
    G = rows // 2
    CW = qkv_raw.shape[2]
    NH = CW // HD
    T = filter_taps.shape[1]
    MR = max(Y, Z) // 2
    nq, nk = Z * G, Y * G
    C = min(256, nq)
    nr = 2 * nq // 128
    raw = jnp.transpose(qkv_raw, (1, 0, 2))
    dma = pltpu.SemaphoreType.DMA
    vmem = pl.BlockSpec(memory_space=pltpu.VMEM)
    attn, grad = pl.pallas_call(
        functools.partial(kernel, (Y, Z, H, G, NH, T)),
        out_shape=(
            jax.ShapeDtypeStruct((rows, CW), BF16),
            jax.ShapeDtypeStruct((3, rows, CW), BF16),
        ),
        in_specs=[vmem, pl.BlockSpec(memory_space=pltpu.SMEM), vmem, vmem],
        out_specs=(vmem, vmem),
        scratch_shapes=[
            pltpu.VMEM((rows, CW), BF16),
            pltpu.VMEM((2, 3, 16, CW), BF16),
            pltpu.VMEM((NH, 2, Z, G, HD), BF16),
            pltpu.VMEM((NH, 2, Z, G, HD), BF16),
            pltpu.VMEM((NH, 2, Y, G, HD), BF16),
            pltpu.VMEM((NH, 2, Y, G, HD), BF16),
            pltpu.VMEM((2, nk, C), jnp.int32),
            pltpu.VMEM((NH, 2 * nk, 2 * nq), F32),
            pltpu.VMEM((NH, 2 * nk, 2 * nq), F32),
            pltpu.VMEM((2 * nk, 2 * nq), BF16),
            pltpu.VMEM((2 * nk, 2 * nq), BF16),
            pltpu.VMEM((NH, Z, 3, nr, 128), F32),
            pltpu.VMEM((NH, nr, 128), F32),
            pltpu.VMEM((NH, nr, 128), F32),
            pltpu.VMEM((NH, 2, Z, G, HD), F32),
            pltpu.VMEM((NH, 2, Z, G, HD), F32),
            pltpu.VMEM((NH, 2, Y, G, HD), F32),
            pltpu.VMEM((NH, 2, Y, G, HD), F32),
            pltpu.VMEM((NH, 4, 2, MR, 2, G, HD), BF16),
            pltpu.VMEM((NH, 4, 2, MR, 2, G, HD), BF16),
            pltpu.VMEM((NH, 3, 2, G, HD), F32),
            pltpu.VMEM((NH, 2, 3, 8, HD), F32),
            pltpu.VMEM((NH, 2, 3, 8, HD), F32),
            dma,
            dma((H - 1,)),
            dma((H - 1,)),
            dma((2,)),
            dma((2,)),
            dma((NH, 4, 2, MR)),
            dma((NH, 4, 2, MR)),
            dma((NH, Z - 1)),
            dma((NH, Z - 1)),
            dma((NH, 4, 2, MR)),
            dma((NH, 4, 2, MR)),
            dma((NH, 2)),
            dma((NH, 2)),
        ],
        compiler_params=pltpu.CompilerParams(
            collective_id=0, has_side_effects=True, vmem_limit_bytes=56 * 1024 * 1024
        ),
    )(raw, positions, filter_taps, grad_out)
    return attn, jnp.transpose(grad, (1, 0, 2))


def solution(mesh):
    n = mesh.shape["ctx"]
    Y = 1
    while (2 * Y) * (2 * Y) <= n and n % (2 * Y) == 0:
        Y *= 2
    in_specs = (P("ctx", None, "head"), P("ctx"), P(None, None, "head"), P(("ctx", "head"), None))
    out_specs = (P("ctx", "head"), P("ctx", None, "head"))
    return jax.shard_map(
        functools.partial(local, Y, n // Y, mesh.shape["head"]),
        mesh=mesh,
        in_specs=in_specs,
        out_specs=out_specs,
        check_vma=False,
    )
```

time: 529 us -> 90.6 us (0.17)
  waiting for transfers between devices: 173 us -> 0 us
  blocking collectives: 122 us -> 0 us
  matrix products: 91.4 us -> 0 us
  Pallas kernels: 0 us -> 86.6 us
  local copies, waits for them, and re-layouts: 75.1 us -> 3.09 us
  starting transfers between devices: 27.5 us -> 0 us
  between operations: 16.8 us -> 0.64 us
  other arithmetic: 15.2 us -> 0 us
    all_gather x4 -> x0, waiting for transfers between devices: 156 us -> none  [the longest x1 87.5 us: local(): lax.all_gather(value_rows.reshape(2, group_len, width_now), 'ctx', axis=1...]
    all_gather x2 -> x0, blocking collectives: 122 us -> none  [the longest x1 66.4 us: local(): lax.all_gather(delta.reshape(2, group_len, head_count), 'ctx', axis=1, ti...]
    dot_general x384 -> x0, matrix products: 91.4 us -> none  [the longest x64 14.9 us: split_product(): jnp.einsum('hqk,khd->qhd', low_part, key_rows, preferred_element_type=jnp...]
    pallas_call x0 -> x1, Pallas kernels: none -> 86.6 us  [local(): pl.pallas_call(functools.partial(kernel, (Y, Z, H, G, NH, T)), out_shape=...]
    dynamic_slice x48 -> x0, local copies, waits for them, and re-layouts: 48.5 us -> none  [the longest x16 17.2 us: inner(): lax.dynamic_slice_in_dim(grad_block, begin, step_rows, 1)]
    ppermute x4 -> x0, starting transfers between devices: 22.6 us -> none  [the longest x2 18.4 us: extended_2(): lax.ppermute(head, axis, [((i + 1) % count, i) for i in range(count)])]
    ppermute x4 -> x0, waiting for transfers between devices: 14.9 us -> none  [the longest x2 13.6 us: extended_2(): lax.ppermute(tail, axis, [(i, (i + 1) % count) for i in range(count)])]
    unnamed x13 -> x2, local copies, waits for them, and re-layouts: 11.5 us -> 3.09 us
  transfers between devices with their start and end apart: 9 -> 0, of which waited for: 6 -> 0; matrix products, arithmetic and copies ran while one was open for 25% -> 0% of each run, Pallas kernels for 0% -> 0%
where the time goes in v1:
time: 90.6 us; the launch traced here: 90.4 us
  Pallas kernels  86.6 us (96%)
  local copies, waits for them, and re-layouts  3.09 us (3%)
    pallas_call x1, Pallas kernels, local(): pl.pallas_call(functools.partial(kernel, (Y, Z, H, G, NH, T)), out_shape=...  86.6 us
    unnamed x2, local copies, waits for them, and re-layouts  3.09 us

profile of v1, /device:TPU:6, one launch (start us, length us, event | category | flops | bytes accessed | tf_op | source)
XLA Modules:
  0.0 90.4 jit_solution(7547665387437415982)
XLA Ops:
  0.6 86.6 %shard_map.59 = (bf16[128,256]{1,0:T(8,128)(2,1)}, bf16[3,128,256]{2,1,0:T(8,128)(2,1)}) custom-call(bf16[3,128,256]{2,1,0:T(8,128)(2,1)} %bitcast.3, s32[128]{0:T(128)} %pos_ref.1, f32[3,3,256]{2,1,0:T(4,128)} %taps_ref.1, bf16[16,2048]{1,0:T(8,128)(2,1)} %gout_ref.1), custom_call_target="tpu_custom_call" | custom-call | tf_op jit(solution)/shard_map/pallas_call | solution.py:493
  87.3 1.5 %copy.8 = bf16[128,256]{1,0:T(8,128)(2,1)} copy(bf16[128,256]{1,0:T(8,128)(2,1)} %get-tuple-element.8) | data formatting | bytes 131072
  88.8 1.6 %copy.9 = bf16[128,3,256]{2,0,1:T(8,128)(2,1)} copy(bf16[128,3,256]{2,0,1:T(8,128)(2,1)} %bitcast.2) | data formatting | bytes 393216

commit v2 on v1

--- a/solution.py
+++ b/solution.py
@@ -27,8 +27,7 @@
     halo_raw,
     q_all,
     d_all,
-    k_all,
-    v_all,
+    kv_all,
     k_code,
     w_all,
     s_all,
@@ -76,12 +75,11 @@
 
     barrier = pltpu.get_barrier_semaphore()
     greet = [(z_dev((z + j) % Z), hd) for j in range(1, Z)]
-    greet += [(y_dev((y + 1) % Y), hd), (y_dev((y + Y - 1) % Y), hd)]
+    greet += [(y_dev((y + j) % Y), hd) for j in range(1, Y) if j <= 2 or Y - j <= 2]
     greet += [(d_next, hd), (d_prev, hd)]
     greet += [(d, (hd + j) % H) for j in range(1, H)]
     for dev in greet:
         pl.semaphore_signal(barrier, inc=1, device_id=dev, device_id_type=MESH)
-    pl.semaphore_wait(barrier, len(greet))
 
     def remote(src, dst, s_sem, r_sem, dev):
         return pltpu.make_async_remote_copy(
@@ -94,8 +92,6 @@
     tail_l = remote(
         raw_ref.at[:, pl.ds(2 * G - 16, 16)], halo_raw.at[1], hr_send.at[1], hr_recv.at[1], (d_prev, hd)
     )
-    tail_e.start()
-    tail_l.start()
     RB = 2 * G // H
     CW = NH * HD
 
@@ -119,8 +115,6 @@
             (d, frm),
         )
 
-    for j in range(1, H):
-        a2a(j).start()
     own = pltpu.make_async_copy(
         gout_ref.at[:, pl.ds(pl.multiple_of(hd * CW, CW), CW)],
         land.at[pl.ds(pl.multiple_of(hd * RB, RB), RB)],
@@ -133,92 +127,134 @@
     nk = Y * G
     nq = Z * G
     C = min(256, nq)
-    ik = lax.broadcasted_iota(jnp.int32, (nk, C), 0)
-    pk = ((ik // G) * Z + (z + rot)) % N
-    k_code[0] = pk * G + ik % G
-    k_code[1] = ik % G - pk * G
+    group_of = lambda i: i >> (G.bit_length() - 1)
+
+    def wrap(p):
+        p = jnp.where(p >= 2 * N, p - 2 * N, p)
+        return jnp.where(p >= N, p - N, p)
 
     def q_code(half, c):
         iq = lax.broadcasted_iota(jnp.int32, (1, C), 1) + c * C
-        pq = (iq // G + (y * Z + rot)) % N
-        return pq * G + iq % G if half == 0 else iq % G - pq * G
-
-    rings = [
-        (q_all, Z, z, z_dev, 0),
-        (d_all, Z, z, z_dev, 1),
-        (k_all, Y, y, y_dev, 0),
-        (v_all, Y, y, y_dev, 1),
+        pq = wrap(group_of(iq) + (y * Z + rot))
+        return pq * G + (iq & (G - 1)) if half == 0 else (iq & (G - 1)) - pq * G
+
+    E = 16
+    gathers = []
+    for h in range(NH):
+        gathers += [
+            (lambda i, h=h: kv_all.at[0, h, :, i, pl.ds(E, G - E)], Y, y, y_dev),
+            (lambda i, h=h: q_all.at[h, :, i, pl.ds(E, G - E)], Z, z, z_dev),
+            (lambda i, h=h: kv_all.at[1, h, :, i, pl.ds(E, G - E)], Y, y, y_dev),
+            (lambda i, h=h: d_all.at[h, :, i], Z, z, z_dev),
+        ]
+    gathers += [
+        (lambda i: kv_all.at[:, :, :, i, pl.ds(0, E)], Y, y, y_dev),
+        (lambda i: q_all.at[:, :, i, pl.ds(0, E)], Z, z, z_dev),
     ]
+    K_EDGE, Q_EDGE = 4 * NH, 4 * NH + 1
+    flips = (0, 0, 1, 1) * NH + (1, 1)
 
     def steps_of(n, flip):
         a, b = n // 2, n - 1 - n // 2
         return (b, a) if flip else (a, b)
 
-    MR = max(Y, Z) // 2
-
-    def ag_copy(h, item, way, s):
-        buf, n, me, dev_of, flip = rings[item]
+    def ag_copy(item, way, dist, incoming=False):
+        view, n, me, dev_of = gathers[item]
         sign = 1 if way == 0 else n - 1
-        slot = (me + (n - sign) * s) % n
-        dev = (dev_of((me + sign) % n), hd)
+        hop = dist if dist <= 2 else dist - 2
+        if incoming:
+            slot = (me + (n - sign) * dist) % n
+        else:
+            slot = me if dist <= 2 else (me + (n - sign) * 2) % n
+        dev = (dev_of((me + sign * hop) % n), hd)
         return remote(
-            buf.at[h, :, slot], buf.at[h, :, slot], ag_send.at[h, item, way, s], ag_recv.at[h, item, way, s], dev
+            view(slot), view(slot), ag_send.at[item, way, dist - 1], ag_recv.at[item, way, dist - 1], dev
         )
 
-    def ag_wait(h, item, way, s):
-        buf, n, me, dev_of, flip = rings[item]
-        sign = 1 if way == 0 else n - 1
-        slot = (me + (n - sign) * (s + 1)) % n
-        dev = (dev_of((me + sign) % n), hd)
-        remote(
-            buf.at[h, :, slot], buf.at[h, :, slot], ag_send.at[h, item, way, s], ag_recv.at[h, item, way, s], dev
-        ).wait_recv()
-
-    def ag_round(h, s, items=(2, 0, 3, 1)):
-        for item in items:
-            n, flip = rings[item][1], rings[item][4]
-            steps = steps_of(n, flip)
-            for way in range(2):
-                if 0 < s <= steps[way]:
-                    ag_wait(h, item, way, s - 1)
-                if s < steps[way]:
-                    ag_copy(h, item, way, s).start()
-
-    tail_e.wait_recv()
-    tail_l.wait_recv()
-    row = lax.broadcasted_iota(jnp.int32, (G, CW), 0)
+    def ag_counts(item):
+        return enumerate(steps_of(gathers[item][1], flips[item]))
+
+    def ag_first(item):
+        for dist in (2, 1):
+            for way, count in ag_counts(item):
+                if dist <= count:
+                    ag_copy(item, way, dist).start()
+
+    def ag_relay(item):
+        for way, count in ag_counts(item):
+            if count >= 2:
+                ag_copy(item, way, 2, True).wait_recv()
+            for dist in (4, 3):
+                if dist <= count:
+                    ag_copy(item, way, dist).start()
+
+    def ag_last(item):
+        for way, count in ag_counts(item):
+            for dist in (1, 3, 4):
+                if dist <= count:
+                    ag_copy(item, way, dist, True).wait_recv()
+
     zero_rows = jnp.zeros((16, CW), F32)
 
-    def featurize(kind, half):
-        x = raw_ref[kind, pl.ds(half * G, G)].astype(F32)
-        if half == 0:
-            prior = jnp.where(pair == 0, zero_rows, halo_raw[0, kind].astype(F32))
-        else:
-            prior = jnp.where(
-                pair == N - 1, raw_ref[kind, pl.ds(G - 16, 16)].astype(F32), halo_raw[1, kind].astype(F32)
-            )
+    def featurize(kind, half, prior, rows):
+        x = raw_ref[kind, pl.ds(half * G, rows)].astype(F32)
+        row = lax.broadcasted_iota(jnp.int32, (rows, CW), 0)
         tap = taps_ref[kind]
         out = tap[0:1] * x
         for t in range(1, T):
             moved = pltpu.roll(x, t, 0)
-            for i in range(t):
-                moved = jnp.where(row == i, prior[16 - t + i : 17 - t + i], moved)
+            if prior is not None:
+                for i in range(t):
+                    moved = jnp.where(row == i, prior[16 - t + i : 17 - t + i], moved)
             out = out + tap[t : t + 1] * moved
         return out.astype(BF16)
 
-    for kind, buf, slot in ((1, k_all, y), (0, q_all, z), (2, v_all, y)):
+    def own_view(kind, h, half):
+        return q_all.at[h, half, z] if kind == 0 else kv_all.at[kind - 1, h, half, y]
+
+    for kind in (1, 0, 2):
         for half in range(2):
-            out = featurize(kind, half)
+            out = featurize(kind, half, None, G)
             for h in range(NH):
-                buf[h, half, slot] = out[:, h * HD : (h + 1) * HD]
-        ag_round(0, 0, ((1, 2), (0, 0), (2, 3))[(1, 0, 2).index(kind)][1:])
+                own_view(kind, h, half)[pl.ds(E, G - E)] = out[E:, h * HD : (h + 1) * HD]
+
+    pl.semaphore_wait(barrier, len(greet))
+    tail_e.start()
+    tail_l.start()
+    for j in range(1, H):
+        a2a(j).start()
+    for h in range(NH):
+        for item in range(3):
+            ag_first(4 * h + item)
+
+    tail_e.wait_recv()
+    tail_l.wait_recv()
+    for kind in range(3):
+        for half in range(2):
+            if half == 0:
+                prior = jnp.where(pair == 0, zero_rows, halo_raw[0, kind].astype(F32))
+            else:
+                prior = jnp.where(
+                    pair == N - 1, raw_ref[kind, pl.ds(G - 16, 16)].astype(F32), halo_raw[1, kind].astype(F32)
+                )
+            out = featurize(kind, half, prior, E)
+            for h in range(NH):
+                own_view(kind, h, half)[pl.ds(0, E)] = out[:, h * HD : (h + 1) * HD]
+    ag_first(K_EDGE)
+    ag_first(Q_EDGE)
     own.wait()
     for j in range(1, H):
         a2a_in(j).wait_recv()
     for half in range(2):
         for h in range(NH):
             d_all[h, half, z] = land[pl.ds(half * G, G), h * HD : (h + 1) * HD]
-    ag_round(0, 0, (1,))
+    for h in range(NH):
+        ag_first(4 * h + 3)
+
+    ik = lax.broadcasted_iota(jnp.int32, (nk, C), 0)
+    pk = wrap(group_of(ik) * Z + (z + rot))
+    k_code[0] = pk * G + (ik & (G - 1))
+    k_code[1] = (ik & (G - 1)) - pk * G
 
     NT = (((1,), (1,)), ((), ()))
     TN = (((0,), (0,)), ((), ()))
@@ -237,7 +273,7 @@
         tops = []
         score = []
         for kh in range(half + 1):
-            keys = k_all[h, kh].reshape(nk, HD)
+            keys = kv_all[0, h, kh].reshape(nk, HD)
             sc = mm(keys, q, NT)
             if kh == half:
                 sc = jnp.where(k_code[half] <= q_code(half, c), sc, NEG)
@@ -249,7 +285,7 @@
         for kh in range(half + 1):
             w = jnp.exp2((score[kh] - top) * cexp)
             w_all[h, pl.ds(kh * nk, nk), cols] = w
-            slope = mm(v_all[h, kh].reshape(nk, HD), g, NT)
+            slope = mm(kv_all[1, h, kh].reshape(nk, HD), g, NT)
             s_all[h, pl.ds(kh * nk, nk), cols] = slope
             total = total + jnp.sum(w, axis=0, keepdims=True)
             tilt = tilt + jnp.sum(w * slope, axis=0, keepdims=True)
@@ -315,11 +351,11 @@
         ks = pl.ds(0, nk * (half + 1))
         cols = pl.ds(half * nq, nq)
         if half == 0:
-            k = k_all[h, 0].reshape(nk, HD)
-            v = v_all[h, 0].reshape(nk, HD)
+            k = kv_all[0, h, 0].reshape(nk, HD)
+            v = kv_all[1, h, 0].reshape(nk, HD)
         else:
-            k = k_all[h].reshape(2 * nk, HD)
-            v = v_all[h].reshape(2 * nk, HD)
+            k = kv_all[0, h].reshape(2 * nk, HD)
+            v = kv_all[1, h].reshape(2 * nk, HD)
         part_o[h, half] = mm(p_low[ks, cols], v, TN).reshape(Z, G, HD)
         part_q[h, half] = (mm(x_low[ks, cols], k, TN) * scaling).reshape(Z, G, HD)
 
@@ -330,41 +366,53 @@
         (part_v, Y, y, y_dev, 1),
     ]
 
-    def rs_copy(h, item, way, s):
+    def rs_copy(h, item, way, dist):
         part, n, me, dev_of, flip = rs_rings[item]
         sign = 1 if way == 0 else n - 1
+        hop = dist if dist <= 2 else dist - 2
         return remote(
-            rs_out.at[h, item, way, s],
-            rs_in.at[h, item, way, s],
-            rs_send.at[h, item, way, s],
-            rs_recv.at[h, item, way, s],
-            (dev_of((me + sign) % n), hd),
+            rs_out.at[h, item, way, dist - 1],
+            rs_in.at[h, item, way, dist - 1],
+            rs_send.at[h, item, way, dist - 1],
+            rs_recv.at[h, item, way, dist - 1],
+            (dev_of((me + sign * hop) % n), hd),
         )
 
-    def rs_round(h, s, items=(2, 0, 3, 1)):
-        for item in items:
-            part, n, me, dev_of, flip = rs_rings[item]
-            steps = steps_of(n, flip)
-            for way in range(2):
-                count = steps[way]
-                if s < count:
-                    sign = 1 if way == 0 else n - 1
-                    dest = (me + sign * (count - s)) % n
-                    val = part[h, :, pl.ds(dest, 1)].reshape(2, G, HD)
-                    if s > 0:
-                        rs_copy(h, item, way, s - 1).wait_recv()
-                        val = val + rs_in[h, item, way, s - 1].astype(F32)
-                    rs_out[h, item, way, s] = val.astype(BF16)
-                    rs_copy(h, item, way, s).start()
+    def rs_counts(item):
+        return enumerate(steps_of(rs_rings[item][1], rs_rings[item][4]))
+
+    def rs_put(h, item, way, dist):
+        part, n, me, dev_of, flip = rs_rings[item]
+        sign = 1 if way == 0 else n - 1
+        val = part[h, :, pl.ds((me + sign * dist) % n, 1)].reshape(2, G, HD)
+        if dist == 2:
+            count = steps_of(n, flip)[way]
+            for more in (3, 4):
+                if more <= count:
+                    rs_copy(h, item, way, more).wait_recv()
+                    val = val + rs_in[h, item, way, more - 1].astype(F32)
+        rs_out[h, item, way, dist - 1] = val.astype(BF16)
+        rs_copy(h, item, way, dist).start()
+
+    def rs_first(h, item):
+        for dist in (4, 3, 1):
+            for way, count in rs_counts(item):
+                if dist <= count:
+                    rs_put(h, item, way, dist)
+
+    def rs_relay(h, item):
+        for way, count in rs_counts(item):
+            if count >= 2:
+                rs_put(h, item, way, 2)
 
     def rs_final(h, item):
         part, n, me, dev_of, flip = rs_rings[item]
-        steps = steps_of(n, flip)
         val = part[h, :, pl.ds(me, 1)].reshape(2, G, HD)
-        for way in range(2):
-            if steps[way] > 0:
-                rs_copy(h, item, way, steps[way] - 1).wait_recv()
-                val = val + rs_in[h, item, way, steps[way] - 1].astype(F32)
+        for way, count in rs_counts(item):
+            for dist in (1, 2):
+                if dist <= count:
+                    rs_copy(h, item, way, dist).wait_recv()
+                    val = val + rs_in[h, item, way, dist - 1].astype(F32)
         return val
 
     def hg_copy(h, half):
@@ -412,20 +460,18 @@
     nc = nq // C
     kc = nk // KC
     chunks = [(1, c) for c in range(nc)] + [(0, c) for c in range(nc)]
-    for s in range(1, MR + 1):
-        if s == min(3, MR):
-            ag_round(1, 0)
-        ag_round(0, s)
-    done = 1
-    for half, c in chunks:
-        if done < MR:
-            ag_round(1, done)
-            done += 1
+    for item in (0, 1, 2, 4, 5, 6, K_EDGE, Q_EDGE, 3):
+        ag_relay(item)
+    for item in (0, 1, 2, K_EDGE, Q_EDGE, 3):
+        ag_last(item)
+    for half, c in chunks[:nc]:
         pass1(0, half, c)
-    while done <= MR:
-        ag_round(1, done)
-        done += 1
+    ag_relay(7)
+    for half, c in chunks[nc:]:
+        pass1(0, half, c)
     st_start(0)
+    for item in (4, 5, 6, 7):
+        ag_last(item)
     for half, c in chunks:
         pass1(1, half, c)
     st_start(1)
@@ -433,28 +479,29 @@
     for kh in range(2):
         for c in range(kc):
             pass2_keys(0, kh, c)
-    rs_round(0, 0, (2, 3))
+    rs_first(0, 2)
+    rs_first(0, 3)
     for half in range(2):
         pass2_queries(0, half)
-    rs_round(0, 0, (0, 1))
+    rs_first(0, 1)
+    rs_first(0, 0)
     st_finish(1)
-    done = 1
     for kh in range(2):
         for c in range(kc):
             pass2_keys(1, kh, c)
-            if done < MR:
-                rs_round(0, done)
-                done += 1
-    rs_round(1, 0, (2, 3))
+    rs_first(1, 2)
+    rs_first(1, 3)
+    rs_relay(0, 2)
+    rs_relay(0, 3)
     for half in range(2):
         pass2_queries(1, half)
-    rs_round(1, 0, (0, 1))
-    while done < MR:
-        rs_round(0, done)
-        done += 1
+    rs_first(1, 1)
+    rs_first(1, 0)
+    rs_relay(0, 1)
+    rs_relay(0, 0)
+    for item in (2, 3, 1, 0):
+        rs_relay(1, item)
     finish_sums(0)
-    for s in range(1, MR):
-        rs_round(1, s)
     finish_sums(1)
     finish_grads(0)
     finish_grads(1)
@@ -463,18 +510,24 @@
     tail_l.wait_send()
     for j in range(1, H):
         a2a(j).wait_send()
+    for item in range(len(gathers)):
+        for way, count in ag_counts(item):
+            for dist in range(1, count + 1):
+                ag_copy(item, way, dist).wait_send()
     for h in range(NH):
         for item in range(4):
-            n, flip = rings[item][1], rings[item][4]
-            steps = steps_of(n, flip)
-            for way in range(2):
-                for s in range(steps[way]):
-                    ag_copy(h, item, way, s).wait_send()
-                    rs_copy(h, item, way, s).wait_send()
+            for way, count in rs_counts(item):
+                for dist in range(1, count + 1):
+                    rs_copy(h, item, way, dist).wait_send()
         for j in range(1, Z):
             st_copy(h, j).wait_send()
         for half in range(2):
             hg_copy(h, half).wait_send()
+
+
+def hand_on(attn_in, grad_in, attn_out, grad_out):
+    attn_out[...] = attn_in[...]
+    grad_out[...] = grad_in[...]
 
 
 def local(Y, Z, H, qkv_raw, positions, filter_taps, grad_out):
@@ -503,8 +556,7 @@
             pltpu.VMEM((2, 3, 16, CW), BF16),
             pltpu.VMEM((NH, 2, Z, G, HD), BF16),
             pltpu.VMEM((NH, 2, Z, G, HD), BF16),
-            pltpu.VMEM((NH, 2, Y, G, HD), BF16),
-            pltpu.VMEM((NH, 2, Y, G, HD), BF16),
+            pltpu.VMEM((2, NH, 2, Y, G, HD), BF16),
             pltpu.VMEM((2, nk, C), jnp.int32),
             pltpu.VMEM((NH, 2 * nk, 2 * nq), F32),
             pltpu.VMEM((NH, 2 * nk, 2 * nq), F32),
@@ -527,8 +579,8 @@
             dma((H - 1,)),
             dma((2,)),
             dma((2,)),
-            dma((NH, 4, 2, MR)),
-            dma((NH, 4, 2, MR)),
+            dma((4 * NH + 2, 2, MR)),
+            dma((4 * NH + 2, 2, MR)),
             dma((NH, Z - 1)),
             dma((NH, Z - 1)),
             dma((NH, 4, 2, MR)),
@@ -540,6 +592,15 @@
             collective_id=0, has_side_effects=True, vmem_limit_bytes=56 * 1024 * 1024
         ),
     )(raw, positions, filter_taps, grad_out)
+    attn, grad = pl.pallas_call(
+        hand_on,
+        out_shape=(
+            jax.ShapeDtypeStruct((rows, CW), BF16),
+            jax.ShapeDtypeStruct((3, rows, CW), BF16),
+        ),
+        in_specs=[vmem, vmem],
+        out_specs=(vmem, vmem),
+    )(attn, grad)
     return attn, jnp.transpose(grad, (1, 0, 2))
 
 

time: 90.6 us -> 66.1 us (0.73)
  Pallas kernels: 86.6 us -> 65.3 us
  local copies, waits for them, and re-layouts: 3.09 us -> 0 us
    pallas_call x1, Pallas kernels: 86.6 us -> 63.6 us  [local(): pl.pallas_call(functools.partial(kernel, (Y, Z, H, G, NH, T)), out_shape=...]
    unnamed x2 -> x0, local copies, waits for them, and re-layouts: 3.09 us -> none
    pallas_call x0 -> x1, Pallas kernels: none -> 1.67 us  [local(): pl.pallas_call(hand_on, out_shape=(jax.ShapeDtypeStruct((rows, CW), BF16)...]
where the time goes in v2:
time: 66.1 us; the launch traced here: 65.9 us
  Pallas kernels  65.3 us (99%)
    pallas_call x1, Pallas kernels, local(): pl.pallas_call(functools.partial(kernel, (Y, Z, H, G, NH, T)), out_shape=...  63.6 us
    pallas_call x1, Pallas kernels, local(): pl.pallas_call(hand_on, out_shape=(jax.ShapeDtypeStruct((rows, CW), BF16)...  1.67 us

profile of v2, /device:TPU:6, one launch (start us, length us, event | category | flops | bytes accessed | tf_op | source)
XLA Modules:
  0.0 65.9 jit_solution(1892660211870064192)
XLA Ops:
  0.6 63.6 %shard_map.59 = (bf16[128,256]{1,0:T(8,128)(2,1)}, bf16[3,128,256]{2,1,0:T(8,128)(2,1)}) custom-call(bf16[3,128,256]{2,1,0:T(8,128)(2,1)} %bitcast.2, s32[128]{0:T(128)} %pos_ref.1, f32[3,3,256]{2,1,0:T(4,128)} %taps_ref.1, bf16[16,2048]{1,0:T(8,128)(2,1)} %gout_ref.1), custom_call_target="tpu_custom_call" | custom-call | tf_op jit(solution)/shard_map/pallas_call | solution.py:546
  64.2 1.7 %shard_map.60 = (bf16[128,256]{1,0:T(8,128)(2,1)}, bf16[3,128,256]{2,1,0:T(8,128)(2,1)}) custom-call(bf16[128,256]{1,0:T(8,128)(2,1)} %get-tuple-element.6.attn_in, bf16[3,128,256]{2,1,0:T(8,128)(2,1)} %get-tuple-element.7.grad_in), custom_call_target="tpu_custom_call" | custom-call | tf_op jit(solution)/shard_map/pallas_call | solution.py:595

commit v3 on v2

--- a/solution.py
+++ b/solution.py
@@ -17,12 +17,15 @@
 
 def kernel(
     dims,
+    raw_hbm,
+    pos_hbm,
+    taps_hbm,
+    gout_ref,
+    attn_ref,
+    grad_ref,
     raw_ref,
     pos_ref,
     taps_ref,
-    gout_ref,
-    attn_ref,
-    grad_ref,
     land,
     halo_raw,
     q_all,
@@ -33,18 +36,21 @@
     s_all,
     p_low,
     x_low,
-    stats,
+    stat_ml,
+    stat_t,
+    row_wt,
     row_fac,
     row_del,
-    part_o,
-    part_q,
-    part_k,
-    part_v,
+    part_z,
+    part_y,
     rs_out,
     rs_in,
+    edge_out,
+    edge_in,
     fin,
     halo_out,
     halo_in,
+    load_sem,
     own_sem,
     a2a_send,
     a2a_recv,
@@ -81,16 +87,24 @@
     for dev in greet:
         pl.semaphore_signal(barrier, inc=1, device_id=dev, device_id_type=MESH)
 
+    loads = [
+        pltpu.make_async_copy(raw_hbm, raw_ref, load_sem.at[0]),
+        pltpu.make_async_copy(taps_hbm, taps_ref, load_sem.at[1]),
+        pltpu.make_async_copy(pos_hbm, pos_ref, load_sem.at[2]),
+    ]
+    for load in loads:
+        load.start()
+
     def remote(src, dst, s_sem, r_sem, dev):
         return pltpu.make_async_remote_copy(
             src_ref=src, dst_ref=dst, send_sem=s_sem, recv_sem=r_sem, device_id=dev, device_id_type=MESH
         )
 
     tail_e = remote(
-        raw_ref.at[:, pl.ds(G - 16, 16)], halo_raw.at[0], hr_send.at[0], hr_recv.at[0], (d_next, hd)
+        raw_hbm.at[:, pl.ds(G - 16, 16)], halo_raw.at[0], hr_send.at[0], hr_recv.at[0], (d_next, hd)
     )
     tail_l = remote(
-        raw_ref.at[:, pl.ds(2 * G - 16, 16)], halo_raw.at[1], hr_send.at[1], hr_recv.at[1], (d_prev, hd)
+        raw_hbm.at[:, pl.ds(2 * G - 16, 16)], halo_raw.at[1], hr_send.at[1], hr_recv.at[1], (d_prev, hd)
     )
     RB = 2 * G // H
     CW = NH * HD
@@ -121,6 +135,14 @@
         own_sem,
     )
     own.start()
+
+    pl.semaphore_wait(barrier, len(greet))
+    tail_e.start()
+    tail_l.start()
+    for j in range(1, H):
+        a2a(j).start()
+    for load in loads:
+        load.wait()
 
     pair = pos_ref[0] // G
     rot = (pair - d + N) % N
@@ -152,7 +174,7 @@
         (lambda i: q_all.at[:, :, i, pl.ds(0, E)], Z, z, z_dev),
     ]
     K_EDGE, Q_EDGE = 4 * NH, 4 * NH + 1
-    flips = (0, 0, 1, 1) * NH + (1, 1)
+    flips = [(h + f) % 2 for h in range(NH) for f in (0, 0, 1, 1)] + [0, 0]
 
     def steps_of(n, flip):
         a, b = n // 2, n - 1 - n // 2
@@ -218,14 +240,11 @@
             for h in range(NH):
                 own_view(kind, h, half)[pl.ds(E, G - E)] = out[E:, h * HD : (h + 1) * HD]
 
-    pl.semaphore_wait(barrier, len(greet))
-    tail_e.start()
-    tail_l.start()
-    for j in range(1, H):
-        a2a(j).start()
-    for h in range(NH):
-        for item in range(3):
-            ag_first(4 * h + item)
+    for h in range(NH):
+        ag_first(4 * h)
+        ag_first(4 * h + 1)
+    for h in range(NH):
+        ag_first(4 * h + 2)
 
     tail_e.wait_recv()
     tail_l.wait_recv()
@@ -266,60 +285,77 @@
     zc = C // G
     lanes = C // 128
 
-    def pass1(h, half, c):
+    def cols_of(half, c):
+        return pl.ds(half * nq + c * C, C)
+
+    def put_rows(ref, half, c, val):
+        for i in range(lanes):
+            ref[pl.ds((half * nq + c * C) // 128 + i, 1)] = val[:, i * 128 : (i + 1) * 128]
+
+    def pass_score(h, half, c):
         q = q_all[h, half, pl.ds(c * zc, zc)].reshape(C, HD)
-        g = d_all[h, half, pl.ds(c * zc, zc)].reshape(C, HD)
-        cols = pl.ds(half * nq + c * C, C)
-        tops = []
         score = []
         for kh in range(half + 1):
-            keys = kv_all[0, h, kh].reshape(nk, HD)
-            sc = mm(keys, q, NT)
+            sc = mm(kv_all[0, h, kh].reshape(nk, HD), q, NT)
             if kh == half:
                 sc = jnp.where(k_code[half] <= q_code(half, c), sc, NEG)
             score.append(sc)
-            tops.append(jnp.max(sc, axis=0, keepdims=True))
-        top = tops[0] if half == 0 else jnp.maximum(tops[0], tops[1])
+        top = jnp.max(score[0], axis=0, keepdims=True)
+        if half == 1:
+            top = jnp.maximum(top, jnp.max(score[1], axis=0, keepdims=True))
         total = jnp.zeros((1, C), F32)
+        for kh in range(half + 1):
+            w = jnp.exp2((score[kh] - top) * cexp)
+            w_all[h, pl.ds(kh * nk, nk), cols_of(half, c)] = w
+            total = total + jnp.sum(w, axis=0, keepdims=True)
+        put_rows(stat_ml.at[h, z, 0], half, c, top)
+        put_rows(stat_ml.at[h, z, 1], half, c, total)
+
+    def pass_slope(h, half, c):
+        g = d_all[h, half, pl.ds(c * zc, zc)].reshape(C, HD)
         tilt = jnp.zeros((1, C), F32)
         for kh in range(half + 1):
-            w = jnp.exp2((score[kh] - top) * cexp)
-            w_all[h, pl.ds(kh * nk, nk), cols] = w
             slope = mm(kv_all[1, h, kh].reshape(nk, HD), g, NT)
-            s_all[h, pl.ds(kh * nk, nk), cols] = slope
-            total = total + jnp.sum(w, axis=0, keepdims=True)
+            s_all[h, pl.ds(kh * nk, nk), cols_of(half, c)] = slope
+            w = w_all[h, pl.ds(kh * nk, nk), cols_of(half, c)]
             tilt = tilt + jnp.sum(w * slope, axis=0, keepdims=True)
-        for i in range(lanes):
-            r = (half * nq + c * C) // 128 + i
-            for what, val in enumerate((top, total, tilt)):
-                stats[h, z, what, pl.ds(r, 1)] = val[:, i * 128 : (i + 1) * 128]
-
-    def st_copy(h, j, incoming=False):
+        put_rows(stat_t.at[h, z], half, c, tilt)
+
+    def st_copy(which, h, j, incoming=False):
         slot = (z + Z - j) % Z if incoming else z
         dev = z_dev((z + Z - j) % Z if incoming else (z + j) % Z)
-        return remote(stats.at[h, slot], stats.at[h, slot], st_send.at[h, j - 1], st_recv.at[h, j - 1], (dev, hd))
-
-    def st_start(h):
+        ref = (stat_ml if which == 0 else stat_t).at[h, slot]
+        return remote(ref, ref, st_send.at[which, h, j - 1], st_recv.at[which, h, j - 1], (dev, hd))
+
+    def st_start(which, h):
+        for j in sorted(range(1, Z), key=lambda j: -min(j, Z - j)):
+            st_copy(which, h, j).start()
+
+    def st_wait(which, h):
         for j in range(1, Z):
-            st_copy(h, j).start()
-
-    def st_finish(h):
-        for j in range(1, Z):
-            st_copy(h, j, True).wait_recv()
-        top = stats[h, 0, 0]
+            st_copy(which, h, j, True).wait_recv()
+
+    def st_finish_ml(h):
+        st_wait(0, h)
+        top = stat_ml[h, 0, 0]
         for i in range(1, Z):
-            top = jnp.maximum(top, stats[h, i, 0])
+            top = jnp.maximum(top, stat_ml[h, i, 0])
         total = jnp.zeros_like(top)
-        tilt = jnp.zeros_like(top)
+        rise = []
         for i in range(Z):
-            e = jnp.exp2((stats[h, i, 0] - top) * cexp)
-            total = total + stats[h, i, 1] * e
-            tilt = tilt + stats[h, i, 2] * e
+            rise.append(jnp.exp2((stat_ml[h, i, 0] - top) * cexp))
+            total = total + stat_ml[h, i, 1] * rise[i]
         inv = 1.0 / total
-        row_fac[h] = jnp.exp2((stats[h, z, 0] - top) * cexp) * inv
-        row_del[h] = tilt * inv
-
-    nr = 2 * nq // 128
+        for i in range(Z):
+            row_wt[h, i] = rise[i] * inv
+        row_fac[h] = row_wt[h, z]
+
+    def st_finish_t(h):
+        st_wait(1, h)
+        tilt = stat_t[h, 0] * row_wt[h, 0]
+        for i in range(1, Z):
+            tilt = tilt + stat_t[h, i] * row_wt[h, i]
+        row_del[h] = tilt
 
     def row_of(ref, h, a, b):
         return jnp.concatenate([ref[h, pl.ds(i, 1)] for i in range(a // 128, b // 128)], axis=1)
@@ -327,92 +363,118 @@
     KC = min(256, nk)
     kz = KC // G
 
-    def pass2_keys(h, kh, c):
-        rows = pl.ds(kh * nk + c * KC, KC)
+    def key_block(kh, c):
         lo = 0 if kh == 0 else nq
-        cols = pl.ds(lo, 2 * nq - lo)
-        fac = row_of(row_fac, h, lo, 2 * nq)
-        dl = row_of(row_del, h, lo, 2 * nq)
-        p = w_all[h, rows, cols] * fac
+        return pl.ds(kh * nk + c * KC, KC), lo, pl.ds(lo, 2 * nq - lo)
+
+    def of_queries(buf, h, kh):
+        return buf[h].reshape(2 * nq, HD) if kh == 0 else buf[h, 1].reshape(nq, HD)
+
+    def of_keys(kind, h, half):
+        return kv_all[kind, h].reshape(2 * nk, HD) if half == 1 else kv_all[kind, h, 0].reshape(nk, HD)
+
+    def pass_probs(h, kh, c):
+        rows, lo, cols = key_block(kh, c)
+        p = w_all[h, rows, cols] * row_of(row_fac, h, lo, 2 * nq)
+        w_all[h, rows, cols] = p
         pb = p.astype(BF16)
         p_low[rows, cols] = pb
-        xb = (p * (s_all[h, rows, cols] - dl)).astype(BF16)
+        part_y[1, h, kh, pl.ds(c * kz, kz)] = mm(pb, of_queries(d_all, h, kh), NN).reshape(kz, G, HD)
+
+    def pass_out(h, half):
+        p = p_low[pl.ds(0, nk * (half + 1)), pl.ds(half * nq, nq)]
+        part_z[1, h, half] = mm(p, of_keys(1, h, half), TN).reshape(Z, G, HD)
+
+    def pass_dscores(h, kh, c):
+        rows, lo, cols = key_block(kh, c)
+        x = w_all[h, rows, cols] * (s_all[h, rows, cols] - row_of(row_del, h, lo, 2 * nq))
+        xb = x.astype(BF16)
         x_low[rows, cols] = xb
-        if kh == 0:
-            g = d_all[h].reshape(2 * nq, HD)
-            q = q_all[h].reshape(2 * nq, HD)
-        else:
-            g = d_all[h, 1].reshape(nq, HD)
-            q = q_all[h, 1].reshape(nq, HD)
-        part_v[h, kh, pl.ds(c * kz, kz)] = mm(pb, g, NN).reshape(kz, G, HD)
-        part_k[h, kh, pl.ds(c * kz, kz)] = (mm(xb, q, NN) * scaling).reshape(kz, G, HD)
-
-    def pass2_queries(h, half):
-        ks = pl.ds(0, nk * (half + 1))
-        cols = pl.ds(half * nq, nq)
-        if half == 0:
-            k = kv_all[0, h, 0].reshape(nk, HD)
-            v = kv_all[1, h, 0].reshape(nk, HD)
-        else:
-            k = kv_all[0, h].reshape(2 * nk, HD)
-            v = kv_all[1, h].reshape(2 * nk, HD)
-        part_o[h, half] = mm(p_low[ks, cols], v, TN).reshape(Z, G, HD)
-        part_q[h, half] = (mm(x_low[ks, cols], k, TN) * scaling).reshape(Z, G, HD)
-
-    rs_rings = [
-        (part_o, Z, z, z_dev, 0),
-        (part_q, Z, z, z_dev, 1),
-        (part_k, Y, y, y_dev, 0),
-        (part_v, Y, y, y_dev, 1),
-    ]
+        part_y[0, h, kh, pl.ds(c * kz, kz)] = (mm(xb, of_queries(q_all, h, kh), NN) * scaling).reshape(kz, G, HD)
+
+    def pass_dq(h, half):
+        x = x_low[pl.ds(0, nk * (half + 1)), pl.ds(half * nq, nq)]
+        part_z[0, h, half] = (mm(x, of_keys(0, h, half), TN) * scaling).reshape(Z, G, HD)
+
+    def dq_like(which):
+        return (part_z, Z, z, z_dev) if which == "z" else (part_y, Y, y, y_dev)
+
+    O_ALL, Q_REST, K_REST, V_ALL, DK_EDGE, DQ_EDGE = range(6)
+
+    def sum_of(h, item):
+        r = E if h == NH - 1 else 0
+        a, b = h % 2, (h + 1) % 2
+        return (
+            ("z", 1, 0, G, a),
+            ("z", 0, r, G - r, a),
+            ("y", 0, r, G - r, a),
+            ("y", 1, 0, G, a),
+            ("y", 0, 0, E, b),
+            ("z", 0, 0, E, b),
+        )[item]
+
+    def items_of(h):
+        return range(6 if h == NH - 1 else 4)
+
+    def rs_bufs(h, item, way, dist):
+        which, kind, row0, rows, flip = sum_of(h, item)
+        if item >= DK_EDGE:
+            return edge_out.at[item - DK_EDGE, way, dist - 1], edge_in.at[item - DK_EDGE, way, dist - 1]
+        at = (h, item, way, dist - 1, slice(None), pl.ds(row0, rows))
+        return rs_out.at[at], rs_in.at[at]
 
     def rs_copy(h, item, way, dist):
-        part, n, me, dev_of, flip = rs_rings[item]
+        part, n, me, dev_of = dq_like(sum_of(h, item)[0])
         sign = 1 if way == 0 else n - 1
         hop = dist if dist <= 2 else dist - 2
+        src, dst = rs_bufs(h, item, way, dist)
         return remote(
-            rs_out.at[h, item, way, dist - 1],
-            rs_in.at[h, item, way, dist - 1],
+            src,
+            dst,
             rs_send.at[h, item, way, dist - 1],
             rs_recv.at[h, item, way, dist - 1],
             (dev_of((me + sign * hop) % n), hd),
         )
 
-    def rs_counts(item):
-        return enumerate(steps_of(rs_rings[item][1], rs_rings[item][4]))
+    def rs_counts(h, item):
+        which, kind, row0, rows, flip = sum_of(h, item)
+        return enumerate(steps_of(Z if which == "z" else Y, flip))
+
+    def rs_part(h, item, dest):
+        which, kind, row0, rows, flip = sum_of(h, item)
+        return dq_like(which)[0][kind, h, :, pl.ds(dest, 1), pl.ds(row0, rows)].reshape(2, rows, HD)
 
     def rs_put(h, item, way, dist):
-        part, n, me, dev_of, flip = rs_rings[item]
+        part, n, me, dev_of = dq_like(sum_of(h, item)[0])
         sign = 1 if way == 0 else n - 1
-        val = part[h, :, pl.ds((me + sign * dist) % n, 1)].reshape(2, G, HD)
+        val = rs_part(h, item, (me + sign * dist) % n)
         if dist == 2:
-            count = steps_of(n, flip)[way]
+            count = steps_of(n, sum_of(h, item)[4])[way]
             for more in (3, 4):
                 if more <= count:
                     rs_copy(h, item, way, more).wait_recv()
-                    val = val + rs_in[h, item, way, more - 1].astype(F32)
-        rs_out[h, item, way, dist - 1] = val.astype(BF16)
+                    val = val + rs_bufs(h, item, way, more)[1][...].astype(F32)
+        rs_bufs(h, item, way, dist)[0][...] = val.astype(BF16)
         rs_copy(h, item, way, dist).start()
 
     def rs_first(h, item):
         for dist in (4, 3, 1):
-            for way, count in rs_counts(item):
+            for way, count in rs_counts(h, item):
                 if dist <= count:
                     rs_put(h, item, way, dist)
 
     def rs_relay(h, item):
-        for way, count in rs_counts(item):
+        for way, count in rs_counts(h, item):
             if count >= 2:
                 rs_put(h, item, way, 2)
 
     def rs_final(h, item):
-        part, n, me, dev_of, flip = rs_rings[item]
-        val = part[h, :, pl.ds(me, 1)].reshape(2, G, HD)
-        for way, count in rs_counts(item):
+        val = rs_part(h, item, z if sum_of(h, item)[0] == "z" else y)
+        for way, count in rs_counts(h, item):
             for dist in (1, 2):
                 if dist <= count:
                     rs_copy(h, item, way, dist).wait_recv()
-                    val = val + rs_in[h, item, way, dist - 1].astype(F32)
+                    val = val + rs_bufs(h, item, way, dist)[1][...].astype(F32)
         return val
 
     def hg_copy(h, half):
@@ -424,17 +486,26 @@
             (d_prev if half == 0 else d_next, hd),
         )
 
-    def finish_sums(h):
-        for kind, item in ((0, 1), (1, 2), (2, 3)):
-            val = rs_final(h, item)
-            fin[h, kind] = val
+    def send_halo(h):
+        for kind in range(3):
             for half in range(2):
-                halo_out[h, half, kind] = val[half, 0:8]
+                halo_out[h, half, kind] = fin[h, kind, half, 0:8]
         for half in range(2):
             hg_copy(h, half).start()
-        o = rs_final(h, 0).astype(BF16)
-        for half in range(2):
-            attn_ref[pl.ds(half * G, G), h * HD : (h + 1) * HD] = o[half]
+
+    def finish_edges(h):
+        for kind, item in ((1, DK_EDGE), (0, DQ_EDGE)):
+            fin[h, kind, :, pl.ds(0, E)] = rs_final(h, item)
+
+    def finish_sums(h, items):
+        for item in items:
+            val = rs_final(h, item)
+            if item == O_ALL:
+                for half in range(2):
+                    attn_ref[pl.ds(half * G, G), h * HD : (h + 1) * HD] = val[half].astype(BF16)
+            else:
+                which, kind, row0, rows, flip = sum_of(h, item)
+                fin[h, {Q_REST: 0, K_REST: 1, V_ALL: 2}[item], :, pl.ds(row0, rows)] = val
 
     row1 = lax.broadcasted_iota(jnp.int32, (G, HD), 0)
 
@@ -460,49 +531,58 @@
     nc = nq // C
     kc = nk // KC
     chunks = [(1, c) for c in range(nc)] + [(0, c) for c in range(nc)]
-    for item in (0, 1, 2, 4, 5, 6, K_EDGE, Q_EDGE, 3):
+    for item in (0, 1, 4, 5, 2, 6, K_EDGE, Q_EDGE, 3, 7):
         ag_relay(item)
-    for item in (0, 1, 2, K_EDGE, Q_EDGE, 3):
-        ag_last(item)
-    for half, c in chunks[:nc]:
-        pass1(0, half, c)
-    ag_relay(7)
-    for half, c in chunks[nc:]:
-        pass1(0, half, c)
-    st_start(0)
-    for item in (4, 5, 6, 7):
+    for item in (0, 1, K_EDGE, Q_EDGE):
         ag_last(item)
     for half, c in chunks:
-        pass1(1, half, c)
-    st_start(1)
-    st_finish(0)
-    for kh in range(2):
-        for c in range(kc):
-            pass2_keys(0, kh, c)
-    rs_first(0, 2)
-    rs_first(0, 3)
-    for half in range(2):
-        pass2_queries(0, half)
-    rs_first(0, 1)
-    rs_first(0, 0)
-    st_finish(1)
-    for kh in range(2):
-        for c in range(kc):
-            pass2_keys(1, kh, c)
-    rs_first(1, 2)
-    rs_first(1, 3)
-    rs_relay(0, 2)
-    rs_relay(0, 3)
-    for half in range(2):
-        pass2_queries(1, half)
-    rs_first(1, 1)
-    rs_first(1, 0)
-    rs_relay(0, 1)
-    rs_relay(0, 0)
-    for item in (2, 3, 1, 0):
-        rs_relay(1, item)
-    finish_sums(0)
-    finish_sums(1)
+        pass_score(0, half, c)
+    st_start(0, 0)
+    ag_last(4)
+    ag_last(5)
+    for half, c in chunks:
+        pass_score(1, half, c)
+    st_start(0, 1)
+    for h in range(NH):
+        ag_last(4 * h + 2)
+        ag_last(4 * h + 3)
+        for half, c in chunks:
+            pass_slope(h, half, c)
+        st_start(1, h)
+    for h in range(NH):
+        st_finish_ml(h)
+        for kh in range(2):
+            for c in range(kc):
+                pass_probs(h, kh, c)
+        rs_first(h, V_ALL)
+        for half in range(2):
+            pass_out(h, half)
+        rs_first(h, O_ALL)
+    for h in range(NH):
+        st_finish_t(h)
+        for kh in range(2):
+            for c in range(kc):
+                pass_dscores(h, kh, c)
+        if h == NH - 1:
+            rs_first(h, DK_EDGE)
+        rs_first(h, K_REST)
+        for half in range(2):
+            pass_dq(h, half)
+        if h == NH - 1:
+            rs_first(h, DQ_EDGE)
+        rs_first(h, Q_REST)
+    for h in range(NH):
+        rs_relay(h, V_ALL)
+        rs_relay(h, O_ALL)
+    for h, item in ((0, K_REST), (0, Q_REST), (1, DK_EDGE), (1, DQ_EDGE), (1, K_REST), (1, Q_REST)):
+        rs_relay(h, item)
+    finish_sums(0, (V_ALL, O_ALL))
+    finish_sums(1, (V_ALL, O_ALL))
+    finish_sums(0, (K_REST, Q_REST))
+    send_halo(0)
+    finish_edges(1)
+    send_halo(1)
+    finish_sums(1, (K_REST, Q_REST))
     finish_grads(0)
     finish_grads(1)
 
@@ -515,12 +595,13 @@
             for dist in range(1, count + 1):
                 ag_copy(item, way, dist).wait_send()
     for h in range(NH):
-        for item in range(4):
-            for way, count in rs_counts(item):
+        for item in items_of(h):
+            for way, count in rs_counts(h, item):
                 for dist in range(1, count + 1):
                     rs_copy(h, item, way, dist).wait_send()
         for j in range(1, Z):
-            st_copy(h, j).wait_send()
+            st_copy(0, h, j).wait_send()
+            st_copy(1, h, j).wait_send()
         for half in range(2):
             hg_copy(h, half).wait_send()
 
@@ -549,9 +630,12 @@
             jax.ShapeDtypeStruct((rows, CW), BF16),
             jax.ShapeDtypeStruct((3, rows, CW), BF16),
         ),
-        in_specs=[vmem, pl.BlockSpec(memory_space=pltpu.SMEM), vmem, vmem],
+        in_specs=[pl.BlockSpec(memory_space=pltpu.HBM)] * 4,
         out_specs=(vmem, vmem),
         scratch_shapes=[
+            pltpu.VMEM((3, rows, CW), BF16),
+            pltpu.SMEM((rows,), jnp.int32),
+            pltpu.VMEM(filter_taps.shape, F32),
             pltpu.VMEM((rows, CW), BF16),
             pltpu.VMEM((2, 3, 16, CW), BF16),
             pltpu.VMEM((NH, 2, Z, G, HD), BF16),
@@ -562,18 +646,21 @@
             pltpu.VMEM((NH, 2 * nk, 2 * nq), F32),
             pltpu.VMEM((2 * nk, 2 * nq), BF16),
             pltpu.VMEM((2 * nk, 2 * nq), BF16),
-            pltpu.VMEM((NH, Z, 3, nr, 128), F32),
+            pltpu.VMEM((NH, Z, 2, nr, 128), F32),
+            pltpu.VMEM((NH, Z, nr, 128), F32),
+            pltpu.VMEM((NH, Z, nr, 128), F32),
             pltpu.VMEM((NH, nr, 128), F32),
             pltpu.VMEM((NH, nr, 128), F32),
-            pltpu.VMEM((NH, 2, Z, G, HD), F32),
-            pltpu.VMEM((NH, 2, Z, G, HD), F32),
-            pltpu.VMEM((NH, 2, Y, G, HD), F32),
-            pltpu.VMEM((NH, 2, Y, G, HD), F32),
+            pltpu.VMEM((2, NH, 2, Z, G, HD), F32),
+            pltpu.VMEM((2, NH, 2, Y, G, HD), F32),
             pltpu.VMEM((NH, 4, 2, MR, 2, G, HD), BF16),
             pltpu.VMEM((NH, 4, 2, MR, 2, G, HD), BF16),
+            pltpu.VMEM((2, 2, MR, 2, 16, HD), BF16),
+            pltpu.VMEM((2, 2, MR, 2, 16, HD), BF16),
             pltpu.VMEM((NH, 3, 2, G, HD), F32),
             pltpu.VMEM((NH, 2, 3, 8, HD), F32),
             pltpu.VMEM((NH, 2, 3, 8, HD), F32),
+            dma((3,)),
             dma,
             dma((H - 1,)),
             dma((H - 1,)),
@@ -581,10 +668,10 @@
             dma((2,)),
             dma((4 * NH + 2, 2, MR)),
             dma((4 * NH + 2, 2, MR)),
-            dma((NH, Z - 1)),
-            dma((NH, Z - 1)),
-            dma((NH, 4, 2, MR)),
-            dma((NH, 4, 2, MR)),
+            dma((2, NH, Z - 1)),
+            dma((2, NH, Z - 1)),
+            dma((NH, 6, 2, MR)),
+            dma((NH, 6, 2, MR)),
             dma((NH, 2)),
             dma((NH, 2)),
         ],

time: 66.1 us -> 64.1 us (0.970)
  Pallas kernels: 65.3 us -> 63.4 us
    pallas_call x1, Pallas kernels: 63.6 us -> 61.7 us  [local(): pl.pallas_call(functools.partial(kernel, (Y, Z, H, G, NH, T)), out_shape=...]
where the time goes in v3:
time: 64.1 us; the launch traced here: 64 us
  Pallas kernels  63.4 us (99%)
    pallas_call x1, Pallas kernels, local(): pl.pallas_call(functools.partial(kernel, (Y, Z, H, G, NH, T)), out_shape=...  61.7 us
    pallas_call x1, Pallas kernels, local(): pl.pallas_call(hand_on, out_shape=(jax.ShapeDtypeStruct((rows, CW), BF16)...  1.67 us

profile of v3, /device:TPU:6, one launch (start us, length us, event | category | flops | bytes accessed | tf_op | source)
XLA Modules:
  0.0 64.0 jit_solution(270360415825463480)
XLA Ops:
  0.6 61.7 %shard_map.59 = (bf16[128,256]{1,0:T(8,128)(2,1)}, bf16[3,128,256]{2,1,0:T(8,128)(2,1)}) custom-call(bf16[3,128,256]{2,1,0:T(8,128)(2,1)} %bitcast.2, s32[128]{0:T(128)} %pos_hbm.1, f32[3,3,256]{2,1,0:T(4,128)} %taps_hbm.1, bf16[16,2048]{1,0:T(8,128)(2,1)} %gout_ref.1), custom_call_target="tpu_custom_call" | custom-call | tf_op jit(solution)/shard_map/pallas_call | solution.py:627
  62.3 1.7 %shard_map.60 = (bf16[128,256]{1,0:T(8,128)(2,1)}, bf16[3,128,256]{2,1,0:T(8,128)(2,1)}) custom-call(bf16[128,256]{1,0:T(8,128)(2,1)} %get-tuple-element.6.attn_in, bf16[3,128,256]{2,1,0:T(8,128)(2,1)} %get-tuple-element.7.grad_in), custom_call_target="tpu_custom_call" | custom-call | tf_op jit(solution)/shard_map/pallas_call | solution.py:682

commit v4 on v3

--- a/solution.py
+++ b/solution.py
@@ -81,7 +81,7 @@
 
     barrier = pltpu.get_barrier_semaphore()
     greet = [(z_dev((z + j) % Z), hd) for j in range(1, Z)]
-    greet += [(y_dev((y + j) % Y), hd) for j in range(1, Y) if j <= 2 or Y - j <= 2]
+    greet += [(y_dev((y + j) % Y), hd) for j in range(1, Y)]
     greet += [(d_next, hd), (d_prev, hd)]
     greet += [(d, (hd + j) % H) for j in range(1, H)]
     for dev in greet:
@@ -183,11 +183,12 @@
     def ag_copy(item, way, dist, incoming=False):
         view, n, me, dev_of = gathers[item]
         sign = 1 if way == 0 else n - 1
-        hop = dist if dist <= 2 else dist - 2
+        near = dist <= 2 or item >= K_EDGE
+        hop = dist if near else dist - 2
         if incoming:
             slot = (me + (n - sign) * dist) % n
         else:
-            slot = me if dist <= 2 else (me + (n - sign) * 2) % n
+            slot = me if near else (me + (n - sign) * 2) % n
         dev = (dev_of((me + sign * hop) % n), hd)
         return remote(
             view(slot), view(slot), ag_send.at[item, way, dist - 1], ag_recv.at[item, way, dist - 1], dev
@@ -197,7 +198,7 @@
         return enumerate(steps_of(gathers[item][1], flips[item]))
 
     def ag_first(item):
-        for dist in (2, 1):
+        for dist in (4, 3, 2, 1) if item >= K_EDGE else (2, 1):
             for way, count in ag_counts(item):
                 if dist <= count:
                     ag_copy(item, way, dist).start()
@@ -212,7 +213,7 @@
 
     def ag_last(item):
         for way, count in ag_counts(item):
-            for dist in (1, 3, 4):
+            for dist in (1, 2, 3, 4) if item >= K_EDGE else (1, 3, 4):
                 if dist <= count:
                     ag_copy(item, way, dist, True).wait_recv()
 
@@ -234,17 +235,13 @@
     def own_view(kind, h, half):
         return q_all.at[h, half, z] if kind == 0 else kv_all.at[kind - 1, h, half, y]
 
-    for kind in (1, 0, 2):
+    for item, kind in enumerate((1, 0, 2)):
         for half in range(2):
             out = featurize(kind, half, None, G)
             for h in range(NH):
                 own_view(kind, h, half)[pl.ds(E, G - E)] = out[E:, h * HD : (h + 1) * HD]
-
-    for h in range(NH):
-        ag_first(4 * h)
-        ag_first(4 * h + 1)
-    for h in range(NH):
-        ag_first(4 * h + 2)
+        for h in range(NH):
+            ag_first(4 * h + item)
 
     tail_e.wait_recv()
     tail_l.wait_recv()
@@ -399,34 +396,32 @@
     def dq_like(which):
         return (part_z, Z, z, z_dev) if which == "z" else (part_y, Y, y, y_dev)
 
-    O_ALL, Q_REST, K_REST, V_ALL, DK_EDGE, DQ_EDGE = range(6)
+    O_ALL, Q_REST, K_REST, V_REST, DQ_EDGE, DK_EDGE, DV_EDGE = range(7)
 
     def sum_of(h, item):
-        r = E if h == NH - 1 else 0
         a, b = h % 2, (h + 1) % 2
         return (
             ("z", 1, 0, G, a),
-            ("z", 0, r, G - r, a),
-            ("y", 0, r, G - r, a),
-            ("y", 1, 0, G, a),
+            ("z", 0, E, G - E, a),
+            ("y", 0, E, G - E, a),
+            ("y", 1, E, G - E, a),
+            ("z", 0, 0, E, b),
             ("y", 0, 0, E, b),
-            ("z", 0, 0, E, b),
+            ("y", 1, 0, E, b),
         )[item]
-
-    def items_of(h):
-        return range(6 if h == NH - 1 else 4)
 
     def rs_bufs(h, item, way, dist):
         which, kind, row0, rows, flip = sum_of(h, item)
-        if item >= DK_EDGE:
-            return edge_out.at[item - DK_EDGE, way, dist - 1], edge_in.at[item - DK_EDGE, way, dist - 1]
+        if item >= DQ_EDGE:
+            at = (h, item - DQ_EDGE, way, dist - 1)
+            return edge_out.at[at], edge_in.at[at]
         at = (h, item, way, dist - 1, slice(None), pl.ds(row0, rows))
         return rs_out.at[at], rs_in.at[at]
 
     def rs_copy(h, item, way, dist):
         part, n, me, dev_of = dq_like(sum_of(h, item)[0])
         sign = 1 if way == 0 else n - 1
-        hop = dist if dist <= 2 else dist - 2
+        hop = dist if dist <= 2 or item >= DQ_EDGE else dist - 2
         src, dst = rs_bufs(h, item, way, dist)
         return remote(
             src,
@@ -448,7 +443,7 @@
         part, n, me, dev_of = dq_like(sum_of(h, item)[0])
         sign = 1 if way == 0 else n - 1
         val = rs_part(h, item, (me + sign * dist) % n)
-        if dist == 2:
+        if dist == 2 and item < DQ_EDGE:
             count = steps_of(n, sum_of(h, item)[4])[way]
             for more in (3, 4):
                 if more <= count:
@@ -458,7 +453,7 @@
         rs_copy(h, item, way, dist).start()
 
     def rs_first(h, item):
-        for dist in (4, 3, 1):
+        for dist in (4, 3, 2, 1) if item >= DQ_EDGE else (4, 3, 1):
             for way, count in rs_counts(h, item):
                 if dist <= count:
                     rs_put(h, item, way, dist)
@@ -471,7 +466,7 @@
     def rs_final(h, item):
         val = rs_part(h, item, z if sum_of(h, item)[0] == "z" else y)
         for way, count in rs_counts(h, item):
-            for dist in (1, 2):
+            for dist in (1, 2, 3, 4) if item >= DQ_EDGE else (1, 2):
                 if dist <= count:
                     rs_copy(h, item, way, dist).wait_recv()
                     val = val + rs_bufs(h, item, way, dist)[1][...].astype(F32)
@@ -494,7 +489,7 @@
             hg_copy(h, half).start()
 
     def finish_edges(h):
-        for kind, item in ((1, DK_EDGE), (0, DQ_EDGE)):
+        for kind, item in ((2, DV_EDGE), (1, DK_EDGE), (0, DQ_EDGE)):
             fin[h, kind, :, pl.ds(0, E)] = rs_final(h, item)
 
     def finish_sums(h, items):
@@ -505,7 +500,7 @@
                     attn_ref[pl.ds(half * G, G), h * HD : (h + 1) * HD] = val[half].astype(BF16)
             else:
                 which, kind, row0, rows, flip = sum_of(h, item)
-                fin[h, {Q_REST: 0, K_REST: 1, V_ALL: 2}[item], :, pl.ds(row0, rows)] = val
+                fin[h, {Q_REST: 0, K_REST: 1, V_REST: 2}[item], :, pl.ds(row0, rows)] = val
 
     row1 = lax.broadcasted_iota(jnp.int32, (G, HD), 0)
 
@@ -531,7 +526,7 @@
     nc = nq // C
     kc = nk // KC
     chunks = [(1, c) for c in range(nc)] + [(0, c) for c in range(nc)]
-    for item in (0, 1, 4, 5, 2, 6, K_EDGE, Q_EDGE, 3, 7):
+    for item in (0, 1, 4, 5, 2, 6, 3, 7):
         ag_relay(item)
     for item in (0, 1, K_EDGE, Q_EDGE):
         ag_last(item)
@@ -554,7 +549,8 @@
         for kh in range(2):
             for c in range(kc):
                 pass_probs(h, kh, c)
-        rs_first(h, V_ALL)
+        rs_first(h, DV_EDGE)
+        rs_first(h, V_REST)
         for half in range(2):
             pass_out(h, half)
         rs_first(h, O_ALL)
@@ -563,26 +559,25 @@
         for kh in range(2):
             for c in range(kc):
                 pass_dscores(h, kh, c)
-        if h == NH - 1:
-            rs_first(h, DK_EDGE)
+        rs_first(h, DK_EDGE)
         rs_first(h, K_REST)
         for half in range(2):
             pass_dq(h, half)
-        if h == NH - 1:
-            rs_first(h, DQ_EDGE)
+        rs_first(h, DQ_EDGE)
         rs_first(h, Q_REST)
     for h in range(NH):
-        rs_relay(h, V_ALL)
+        rs_relay(h, V_REST)
         rs_relay(h, O_ALL)
-    for h, item in ((0, K_REST), (0, Q_REST), (1, DK_EDGE), (1, DQ_EDGE), (1, K_REST), (1, Q_REST)):
-        rs_relay(h, item)
-    finish_sums(0, (V_ALL, O_ALL))
-    finish_sums(1, (V_ALL, O_ALL))
-    finish_sums(0, (K_REST, Q_REST))
-    send_halo(0)
-    finish_edges(1)
-    send_halo(1)
-    finish_sums(1, (K_REST, Q_REST))
+    for h in range(NH):
+        rs_relay(h, K_REST)
+        rs_relay(h, Q_REST)
+    for h in range(NH):
+        finish_edges(h)
+        send_halo(h)
+    for h in range(NH):
+        finish_sums(h, (V_REST, O_ALL))
+    for h in range(NH):
+        finish_sums(h, (K_REST, Q_REST))
     finish_grads(0)
     finish_grads(1)
 
@@ -595,7 +590,7 @@
             for dist in range(1, count + 1):
                 ag_copy(item, way, dist).wait_send()
     for h in range(NH):
-        for item in items_of(h):
+        for item in range(7):
             for way, count in rs_counts(h, item):
                 for dist in range(1, count + 1):
                     rs_copy(h, item, way, dist).wait_send()
@@ -655,8 +650,8 @@
             pltpu.VMEM((2, NH, 2, Y, G, HD), F32),
             pltpu.VMEM((NH, 4, 2, MR, 2, G, HD), BF16),
             pltpu.VMEM((NH, 4, 2, MR, 2, G, HD), BF16),
-            pltpu.VMEM((2, 2, MR, 2, 16, HD), BF16),
-            pltpu.VMEM((2, 2, MR, 2, 16, HD), BF16),
+            pltpu.VMEM((NH, 3, 2, MR, 2, 16, HD), BF16),
+            pltpu.VMEM((NH, 3, 2, MR, 2, 16, HD), BF16),
             pltpu.VMEM((NH, 3, 2, G, HD), F32),
             pltpu.VMEM((NH, 2, 3, 8, HD), F32),
             pltpu.VMEM((NH, 2, 3, 8, HD), F32),
@@ -670,8 +665,8 @@
             dma((4 * NH + 2, 2, MR)),
             dma((2, NH, Z - 1)),
             dma((2, NH, Z - 1)),
-            dma((NH, 6, 2, MR)),
-            dma((NH, 6, 2, MR)),
+            dma((NH, 7, 2, MR)),
+            dma((NH, 7, 2, MR)),
             dma((NH, 2)),
             dma((NH, 2)),
         ],

time: 64.1 us -> 62.8 us (0.980)
  Pallas kernels: 63.4 us -> 61.9 us
    pallas_call x1, Pallas kernels: 61.7 us -> 60.3 us  [local(): pl.pallas_call(functools.partial(kernel, (Y, Z, H, G, NH, T)), out_shape=...]
where the time goes in v4:
time: 62.8 us; the launch traced here: 62.6 us
  Pallas kernels  61.9 us (99%)
  between operations  0.64 us (1%)
    pallas_call x1, Pallas kernels, local(): pl.pallas_call(functools.partial(kernel, (Y, Z, H, G, NH, T)), out_shape=...  60.3 us
    pallas_call x1, Pallas kernels, local(): pl.pallas_call(hand_on, out_shape=(jax.ShapeDtypeStruct((rows, CW), BF16)...  1.67 us

profile of v4, /device:TPU:6, one launch (start us, length us, event | category | flops | bytes accessed | tf_op | source)
XLA Modules:
  0.0 62.6 jit_solution(18213465937717630583)
XLA Ops:
  0.6 60.3 %shard_map.59 = (bf16[128,256]{1,0:T(8,128)(2,1)}, bf16[3,128,256]{2,1,0:T(8,128)(2,1)}) custom-call(bf16[3,128,256]{2,1,0:T(8,128)(2,1)} %bitcast.2, s32[128]{0:T(128)} %pos_hbm.1, f32[3,3,256]{2,1,0:T(4,128)} %taps_hbm.1, bf16[16,2048]{1,0:T(8,128)(2,1)} %gout_ref.1), custom_call_target="tpu_custom_call" | custom-call | tf_op jit(solution)/shard_map/pallas_call | solution.py:622
  60.9 1.7 %shard_map.60 = (bf16[128,256]{1,0:T(8,128)(2,1)}, bf16[3,128,256]{2,1,0:T(8,128)(2,1)}) custom-call(bf16[128,256]{1,0:T(8,128)(2,1)} %get-tuple-element.6.attn_in, bf16[3,128,256]{2,1,0:T(8,128)(2,1)} %get-tuple-element.7.grad_in), custom_call_target="tpu_custom_call" | custom-call | tf_op jit(solution)/shard_map/pallas_call | solution.py:677

commit v5 on v4

--- a/solution.py
+++ b/solution.py
@@ -504,10 +504,12 @@
 
     row1 = lax.broadcasted_iota(jnp.int32, (G, HD), 0)
 
-    def finish_grads(h):
+    def wait_halo(h):
         for half in range(2):
             hg_copy(h, half).wait_recv()
-        for kind in range(3):
+
+    def finish_grads(h, kinds):
+        for kind in kinds:
             tap = taps_ref[kind][:, h * HD : (h + 1) * HD]
             for half in range(2):
                 x = fin[h, kind, half]
@@ -577,9 +579,13 @@
     for h in range(NH):
         finish_sums(h, (V_REST, O_ALL))
     for h in range(NH):
-        finish_sums(h, (K_REST, Q_REST))
-    finish_grads(0)
-    finish_grads(1)
+        wait_halo(h)
+        finish_grads(h, (2,))
+    for h in range(NH):
+        finish_sums(h, (K_REST,))
+        finish_grads(h, (1,))
+        finish_sums(h, (Q_REST,))
+        finish_grads(h, (0,))
 
     tail_e.wait_send()
     tail_l.wait_send()

time: 62.8 us -> 63 us (level)
  no operation moved by 1% of the time
where the time goes in v5:
time: 63 us; the launch traced here: 62.7 us
  Pallas kernels  62.1 us (99%)
  between operations  0.64 us (1%)
    pallas_call x1, Pallas kernels, local(): pl.pallas_call(functools.partial(kernel, (Y, Z, H, G, NH, T)), out_shape=...  60.4 us
    pallas_call x1, Pallas kernels, local(): pl.pallas_call(hand_on, out_shape=(jax.ShapeDtypeStruct((rows, CW), BF16)...  1.67 us

profile of v5, /device:TPU:6, one launch (start us, length us, event | category | flops | bytes accessed | tf_op | source)
XLA Modules:
  0.0 62.7 jit_solution(16470838543298078383)
XLA Ops:
  0.6 60.4 %shard_map.59 = (bf16[128,256]{1,0:T(8,128)(2,1)}, bf16[3,128,256]{2,1,0:T(8,128)(2,1)}) custom-call(bf16[3,128,256]{2,1,0:T(8,128)(2,1)} %bitcast.2, s32[128]{0:T(128)} %pos_hbm.1, f32[3,3,256]{2,1,0:T(4,128)} %taps_hbm.1, bf16[16,2048]{1,0:T(8,128)(2,1)} %gout_ref.1), custom_call_target="tpu_custom_call" | custom-call | tf_op jit(solution)/shard_map/pallas_call | solution.py:628
  61.1 1.7 %shard_map.60 = (bf16[128,256]{1,0:T(8,128)(2,1)}, bf16[3,128,256]{2,1,0:T(8,128)(2,1)}) custom-call(bf16[128,256]{1,0:T(8,128)(2,1)} %get-tuple-element.6.attn_in, bf16[3,128,256]{2,1,0:T(8,128)(2,1)} %get-tuple-element.7.grad_in), custom_call_target="tpu_custom_call" | custom-call | tf_op jit(solution)/shard_map/pallas_call | solution.py:683
